TPU v7x, 128 devices: a whole 4x4x4 slice. The times are simulated.
128 devices in a mesh: expert: 64 (over z, y, x), token: 2 (over core).
Axes of the slice: x: 4, y: 4, z: 4, core: 2. Of those that a mesh axis runs over, the one named last changes fastest.
Arguments:
- tokens: bfloat16 [4096, 3584], P('expert', 'token'), may hold values from -6 to 6
- routes: int32 [4096, 8], P('expert'), may hold values from 0 to 63, all different within a row; in each aligned block of 64 rows (0 to 63, 64 to 127, ...) at most 16 rows name the same one
- mixing: float32 [4096, 8], P('expert'), may hold values from 0.05 to 1
- gate_weight: bfloat16 [64, 3584, 1024], P('expert', None, 'token'), may hold values from -0.09375 to 0.09375
- up_weight: bfloat16 [64, 3584, 1024], P('expert', None, 'token'), may hold values from -0.09375 to 0.09375
- down_weight: bfloat16 [64, 1024, 3584], P('expert', None, 'token'), may hold values from -0.1875 to 0.1875
Outputs:
- mixed: bfloat16 [4096, 3584], P('expert', 'token')
- hessian: float32 [64, 1024, 1024], P('expert', 'token')
Inputs may be any that keep to these rules, and one draw needn't show every extreme that they name: `routes`: each row names 8 different experts; among the 64 rows of one device no expert is named by more than 16 rows, and on some device an expert is named by exactly 16 rows; every expert is named by some row.
All inputs are finite; a program needn't handle non-finite values.
Results may differ from a plain program's by a relative error of at most 0.0058.
Values may be sent and summed in bfloat16 or wider, within the bound.
No kernel may reach another device: no remote copies, remote signals or barrier semaphores. Data moves between devices by JAX's collectives and lax.ppermute only.
A program may use at most 128 MiB of HBM per device.

v0:
```python
import jax
import jax.numpy as jnp
from jax import lax
from jax.sharding import PartitionSpec as P


def shards(tokens, routes, mixing, gate_weight, up_weight, down_weight):
    tok_rows = tokens.shape[0]
    feat_width = tokens.shape[1]
    top_count = routes.shape[1]
    expert_count = lax.axis_size("expert")
    capacity = 2 * tok_rows * top_count // expert_count
    slot_total = expert_count * capacity
    flat_ids = routes.reshape(-1)
    chosen = (flat_ids[:, None] == jnp.arange(expert_count, dtype=jnp.int32)[None, :]).astype(
        jnp.int32
    )
    ranks = jnp.cumsum(chosen, axis=0) - chosen
    slots = jnp.sum(ranks * chosen, axis=1)
    counts = jnp.sum(chosen, axis=0)
    target = flat_ids * capacity + slots
    placing = (target[:, None] == jnp.arange(slot_total, dtype=jnp.int32)[None, :]).astype(
        jnp.bfloat16
    )
    placing = jnp.sum(placing.reshape(tok_rows, top_count, slot_total), axis=1)
    outgoing = lax.dot_general(
        placing, tokens, (((0,), (0,)), ((), ())), preferred_element_type=jnp.float32
    )
    outgoing = outgoing.astype(jnp.bfloat16).reshape(expert_count, capacity, feat_width)
    received, got_counts = (
        lax.all_to_all(outgoing, "expert", split_axis=0, concat_axis=0, tiled=True),
        lax.all_to_all(
            counts.astype(jnp.bfloat16), "expert", split_axis=0, concat_axis=0, tiled=True
        ),
    )
    rows_in = received.reshape(slot_total, feat_width)
    row_total = jnp.sum(got_counts.astype(jnp.float32))
    gate_local = gate_weight[0]
    up_local = up_weight[0]
    piece = lax.all_gather(rows_in, "token", axis=1, tiled=True)
    gate = jnp.dot(piece, gate_local, preferred_element_type=jnp.float32)
    upper = jnp.dot(piece, up_local, preferred_element_type=jnp.float32)
    hidden = (jax.nn.silu(gate) * upper).astype(jnp.bfloat16)
    down_local = down_weight[0]
    piece = lax.all_gather(hidden, "token", axis=1, tiled=True)
    out_sum = jnp.dot(piece, down_local, preferred_element_type=jnp.float32)
    outer = lax.dot_general(
        hidden, piece, (((0,), (0,)), ((), ())), preferred_element_type=jnp.float32
    )
    gram = outer
    out_sum, gram = (out_sum, gram)
    hessian = (2.0 / row_total * gram)[None]
    expert_out = out_sum.astype(jnp.bfloat16).reshape(expert_count, capacity, feat_width)
    returned = lax.all_to_all(expert_out, "expert", split_axis=0, concat_axis=0, tiled=True)
    picked = returned.reshape(slot_total, feat_width)[target]
    picked = picked.reshape(tok_rows, top_count, feat_width).astype(jnp.float32)
    mixed = jnp.sum(picked * mixing[:, :, None], axis=1).astype(jnp.bfloat16)
    return (mixed, hessian)


def solution(mesh):
    placed = (
        P("expert", "token"),
        P("expert", None),
        P("expert", None),
        P("expert", None, "token"),
        P("expert", None, "token"),
        P("expert", None, "token"),
    )
    return jax.shard_map(
        shards,
        mesh=mesh,
        in_specs=placed,
        out_specs=(P("expert", "token"), P("expert", "token", None)),
        check_vma=False,
    )
```

profile of v0, /device:TPU:1, one launch (start us, length us, event | category | flops | bytes accessed | tf_op | source)
XLA Modules:
  0.0 198.8 jit_solution(6012494983117020965)
XLA Ops:
  7.2 0.0 copy-start
  7.2 0.0 all-gather.3.cloned.1.call-start
  7.2 0.8 copy.21
  8.0 0.1 eq.43
  8.1 0.1 eq.39
  8.3 1.2 reduce-window.6
  9.5 0.2 slice_reduce_fusion
  9.7 0.2 convert_reduce_fusion
  9.9 0.1 reduce_sum.53
  10.0 0.7 fusion.9
  10.7 0.0 copy-done
  10.7 1.1 convolution_convert_fusion
  11.9 57.3 %all_to_all.16 = bf16[64,16,1792]{2,1,0:T(8,128)(2,1)} all-to-all(bf16[64,16,1792]{2,1,0:T(8,128)(2,1)S(1)} %bitcast.43), channel_id=1, replica_groups=mesh['expert'=64,'token'=2] {'expert'}, dimensions={0} | all-to-all | bytes 7340032 | tf_op jit(solution)/shard_map/all_to_all | solution.py:31
  69.2 0.0 all-gather.3.cloned.1.call-update
  69.2 0.0 all-gather.5.cloned.1.call-start
  69.3 19.5 %all-gather.3.cloned.1.call-done = bf16[1024,3584]{1,0:T(8,128)(2,1)} async-done(((bf16[1024,1792]{1,0:T(8,128)(2,1)}), bf16[1024,3584]{1,0:T(8,128)(2,1)}) %all-gather.3.cloned.1.call-update) | async-done | bytes 7340048 | tf_op jit(solution)/shard_map/all_gather | solution.py:40
  88.8 7.4 %fusion.2 = f32[1024,512]{1,0:T(8,128)S(1)} fusion(bf16[1024,3584]{1,0:T(8,128)(2,1)} %all-gather.3.cloned.1.call-done, bf16[1,3584,512]{2,1,0:T(8,128)(2,1)} %param.10), kind=kOutput, calls=%fused_computation.6 | convolution fusion | flops 3758096384 | bytes 13107200 | tf_op jit(solution)/shard_map/dot_general | solution.py:42
  96.2 5.2 %multiply_convert_fusion = bf16[1024,512]{1,0:T(8,128)(2,1)} fusion(f32[1024,512]{1,0:T(8,128)S(1)} %fusion.2, bf16[1024,3584]{1,0:T(8,128)(2,1)S(1)} %copy-done.4, bf16[1,3584,512]{2,1,0:T(8,128)(2,1)S(1)} %copy-done.5), kind=kOutput, calls=%fused_computation.11 | convolution fusion | flops 3761242112 | bytes 14155776 | tf_op jit(solution)/shard_map/dot_general | solution.py:41
  101.5 0.0 all-gather.5.cloned.1.call-update
  101.5 0.7 copy.26
  102.2 10.1 %all-to-all-start.2 = ((bf16[64,1,1]{2,1,0:T(2,128)(2,1)}), bf16[64,1,1]{2,1,0:T(2,128)(2,1)S(1)}, u32[]{:S(2)}, u32[]{:S(2)}) async-start(bf16[64,1,1]{2,1,0:T(2,128)(2,1)} %copy.26), calls=%async_computation.2 | async-start | bytes 65536 | tf_op jit(solution)/shard_map/all_to_all | solution.py:32
  112.4 3.9 %all-gather.5.cloned.1.call-done = bf16[1024,1024]{1,0:T(8,128)(2,1)} async-done(((bf16[1024,512]{1,0:T(8,128)(2,1)}), bf16[1024,1024]{1,0:T(8,128)(2,1)}) %all-gather.5.cloned.1.call-update) | async-done | bytes 2097168 | tf_op jit(solution)/shard_map/all_gather | solution.py:45
  116.3 8.5 %convolution_convert_fusion.1 = bf16[1024,1792]{1,0:T(8,128)(2,1)} fusion(bf16[1024,1024]{1,0:T(8,128)(2,1)} %all-gather.5.cloned.1.call-done, bf16[1,1024,1792]{2,1,0:T(8,128)(2,1)} %param.11), kind=kOutput, calls=%fused_computation.2 | convolution fusion | flops 3759931392 | bytes 9437184 | tf_op jit(solution)/shard_map/dot_general | solution.py:46
  124.7 0.0 all-to-all-done.2
  124.7 10.8 %all-to-all-start.1 = ((bf16[64,16,1792]{2,1,0:T(8,128)(2,1)}), bf16[64,16,1792]{2,1,0:T(8,128)(2,1)}, u32[]{:S(2)}, u32[]{:S(2)}) async-start(bf16[64,16,1792]{2,1,0:T(8,128)(2,1)} %bitcast.44), calls=%async_computation.1 | async-start | bytes 7340032 | tf_op jit(solution)/shard_map/all_to_all | solution.py:54
  135.6 0.1 mul.48
  135.7 0.1 copy.25
  135.8 0.7 convert_reduce_fusion.1
  137.1 2.6 %multiply_bitcast_fusion = f32[1,512,1024]{2,1,0:T(8,128)} fusion(bf16[1024,512]{1,0:T(8,128)(2,1)S(1)} %copy-done.1, bf16[1024,1024]{1,0:T(8,128)(2,1)S(1)} %copy-done.2, f32[]{:T(128)S(6)} %div.8), kind=kOutput, calls=%fused_computation.10 | convolution fusion | flops 1074266112 | bytes 5242884 | tf_op jit(solution)/shard_map/dot_general | solution.py:47
  139.7 43.5 %all-to-all-done.1 = bf16[64,16,1792]{2,1,0:T(8,128)(2,1)} async-done(((bf16[64,16,1792]{2,1,0:T(8,128)(2,1)}), bf16[64,16,1792]{2,1,0:T(8,128)(2,1)}, u32[]{:S(2)}, u32[]{:S(2)}) %all-to-all-start.1) | async-done | bytes 3670048 | tf_op jit(solution)/shard_map/all_to_all | solution.py:54
  183.2 6.5 %gather_fusion = bf16[512,1792]{1,0:T(8,128)(2,1)S(1)} fusion(bf16[1024,1792]{1,0:T(8,128)(2,1)} %bitcast.7, s32[1024]{0:T(1024)S(1)} %pad_clamp_fusion), kind=kCustom, calls=%fused_computation | custom fusion | bytes 3672064 | tf_op jit(solution)/shard_map/gather | solution.py:55
  189.7 2.3 %fusion = bf16[64,1792]{1,0:T(8,128)(2,1)} fusion(bf16[512,1792]{1,0:T(8,128)(2,1)S(1)} %gather_fusion, f32[64,8]{1,0:T(8,128)S(1)} %copy.25), kind=kLoop, calls=%fused_computation.4 | loop fusion | flops 2637824 | bytes 2066432 | tf_op jit(solution)/shard_map/reduce_sum | solution.py:57
  (17 shorter events, 0.1 us)
Async XLA Ops:
  7.2 3.5 %copy-start = (bf16[64,1792]{1,0:T(8,128)(2,1)S(1)}, bf16[64,1792]{1,0:T(8,128)(2,1)}, u32[]{:S(2)}) copy-start(bf16[64,1792]{1,0:T(8,128)(2,1)} %param.6) | copy-start | bytes 688132
  7.2 81.6 %all-gather.3.cloned.1.call-start = ((), (), s32[]{:S(2)}) async-start(), calls=%async_computation.3 | async-start | bytes 11010048 | tf_op jit(solution)/shard_map/all_gather | solution.py:40
  69.2 47.0 %all-gather.5.cloned.1.call-start = ((), (), s32[]{:S(2)}) async-start(), calls=%async_computation.4 | async-start | bytes 3145728 | tf_op jit(solution)/shard_map/all_gather | solution.py:45
  88.8 7.4 %copy-start.4 = (bf16[1024,3584]{1,0:T(8,128)(2,1)S(1)}, bf16[1024,3584]{1,0:T(8,128)(2,1)}, u32[]{:S(2)}) copy-start(bf16[1024,3584]{1,0:T(8,128)(2,1)} %all-gather.3.cloned.1.call-done) | copy-start | bytes 22020100
  88.8 7.4 %copy-start.5 = (bf16[1,3584,512]{2,1,0:T(8,128)(2,1)S(1)}, bf16[1,3584,512]{2,1,0:T(8,128)(2,1)}, u32[]{:S(2)}) copy-start(bf16[1,3584,512]{2,1,0:T(8,128)(2,1)} %param.9) | copy-start | bytes 11010052
  102.2 22.5 %all-to-all-start.2 = ((bf16[64,1,1]{2,1,0:T(2,128)(2,1)}), bf16[64,1,1]{2,1,0:T(2,128)(2,1)S(1)}, u32[]{:S(2)}, u32[]{:S(2)}) async-start(bf16[64,1,1]{2,1,0:T(2,128)(2,1)} %copy.26), calls=%async_computation.2 | async-start | bytes 65536 | tf_op jit(solution)/shard_map/all_to_all | solution.py:32
  124.7 10.9 %copy-start.3 = (f32[64,8]{0,1:T(8,128)S(1)}, f32[64,8]{0,1:T(8,128)}, u32[]{:S(2)}) copy-start(f32[64,8]{0,1:T(8,128)} %param.8) | copy-start | bytes 6148
  124.7 12.4 %copy-start.1 = (bf16[1024,512]{1,0:T(8,128)(2,1)S(1)}, bf16[1024,512]{1,0:T(8,128)(2,1)}, u32[]{:S(2)}) copy-start(bf16[1024,512]{1,0:T(8,128)(2,1)} %multiply_convert_fusion) | copy-start | bytes 3145732
  124.7 12.4 %copy-start.2 = (bf16[1024,1024]{1,0:T(8,128)(2,1)S(1)}, bf16[1024,1024]{1,0:T(8,128)(2,1)}, u32[]{:S(2)}) copy-start(bf16[1024,1024]{1,0:T(8,128)(2,1)} %all-gather.5.cloned.1.call-done) | copy-start | bytes 6291460
  124.7 58.4 %all-to-all-start.1 = ((bf16[64,16,1792]{2,1,0:T(8,128)(2,1)}), bf16[64,16,1792]{2,1,0:T(8,128)(2,1)}, u32[]{:S(2)}, u32[]{:S(2)}) async-start(bf16[64,16,1792]{2,1,0:T(8,128)(2,1)} %bitcast.44), calls=%async_computation.1 | async-start | bytes 7340032 | tf_op jit(solution)/shard_map/all_to_all | solution.py:54
Sparse Core Ops, SparseCore 0:
  69.4 19.3 all-gather.2
  101.6 14.6 all-gather.4
where the time goes:
time: 199 us
  waiting for transfers between devices  66.9 us (34%)
  blocking collectives  57.3 us (29%)
  matrix products  24.9 us (13%)
  starting transfers between devices  21 us (11%)
  between operations  14.9 us (7%)
  local copies, waits for them, and re-layouts  8.72 us (4%)
  other arithmetic  5.11 us (3%)
    all_to_all x1, blocking collectives, shards(): lax.all_to_all(outgoing, 'expert', split_axis=0, concat_axis=0, tiled=True)  57.3 us
    all_to_all x1, waiting for transfers between devices, shards(): lax.all_to_all(expert_out, 'expert', split_axis=0, concat_axis=0, tiled=T...  43.5 us
    all_gather x1, waiting for transfers between devices, shards(): piece = lax.all_gather(rows_in, 'token', axis=1, tiled=True)  19.5 us
    all_to_all x1, starting transfers between devices, shards(): lax.all_to_all(expert_out, 'expert', split_axis=0, concat_axis=0, tiled=T...  10.8 us
    all_to_all x1, starting transfers between devices, shards(): lax.all_to_all(counts.astype(jnp.bfloat16), 'expert', split_axis=0, conca...  10.1 us
    dot_general x1, matrix products, shards(): out_sum = jnp.dot(piece, down_local, preferred_element_type=jnp.float32)  8.46 us
    dot_general x1, matrix products, shards(): upper = jnp.dot(piece, up_local, preferred_element_type=jnp.float32)  7.42 us
    gather x1, local copies, waits for them, and re-layouts, shards(): picked = returned.reshape(slot_total, feat_width)[target]  6.45 us
  transfers between devices with their start and end apart: 4, of which 3 were waited for; matrix products, arithmetic and copies ran while one was open for 6% of the time, Pallas kernels for 0%

commit v1 on v0

v1 whole, which is shorter than its diff:
```python
import jax
import jax.numpy as jnp
from jax import lax
from jax.experimental import pallas as pl
from jax.experimental.pallas import tpu as pltpu
from jax.sharding import PartitionSpec as P

EMPTY = 64.0


def expert_kernel(
    core_ref, x_hbm, gate_own, up_own, gate_other, up_other, down_own, down_other,
    out_ref, hid_ref, count_ref, x, weights, downs, x_sem, w_sem, d_sem,
):
    core = core_ref[0]
    rows = x.shape[1]
    half = x.shape[2]
    ff_half = gate_own.shape[2]
    tile = weights.shape[3]
    tiles = ff_half // tile
    copies = []
    for f in range(2):
        copy = pltpu.make_async_copy(x_hbm.at[f], x.at[f], x_sem.at[f])
        copy.start()
        copies.append(copy)
    loads = []
    for side, pair in enumerate(((gate_own, up_own), (gate_other, up_other))):
        for j in range(tiles):
            for which, src in enumerate(pair):
                place = (side * tiles + j) * 2 + which
                copy = pltpu.make_async_copy(
                    src.at[0, :, pl.ds(j * tile, tile)], weights.at[place // 2, which], w_sem.at[place]
                )
                copy.start()
                loads.append(copy)
    down_loads = []
    for side, src in enumerate((down_own, down_other)):
        copy = pltpu.make_async_copy(src.at[0], downs.at[side], d_sem.at[side])
        copy.start()
        down_loads.append(copy)
    for copy in copies:
        copy.wait()
    valid = x[0, :, :128].astype(jnp.float32)[:, :1] < EMPTY / 2
    count_ref[...] = jnp.full(count_ref.shape, jnp.sum(valid.astype(jnp.float32)))

    def product(place, which):
        return jnp.dot(
            x[0], weights[place, which, :half], preferred_element_type=jnp.float32
        ) + jnp.dot(x[1], weights[place, which, half:], preferred_element_type=jnp.float32)

    for side in range(2):
        base = (core if side == 0 else 1 - core) * ff_half
        for j in range(tiles):
            place = side * tiles + j
            loads[2 * place].wait()
            loads[2 * place + 1].wait()
            gate = product(place, 0)
            upper = product(place, 1)
            hidden = jnp.where(valid, gate / (1.0 + jnp.exp(-gate)) * upper, 0.0)
            columns = pl.ds(pl.multiple_of(base + j * tile, tile), tile)
            hid_ref[:, columns] = hidden.astype(hid_ref.dtype)
    wide = 256
    for side in range(2):
        down_loads[side].wait()
        target = core if side == 0 else 1 - core
        for n in range(half // wide):
            columns = pl.ds(n * wide, wide)
            out_ref[target, :, columns] = jnp.dot(
                hid_ref[...], downs[side, :, columns], preferred_element_type=jnp.float32
            ).astype(out_ref.dtype)


def run_experts(core, x, gate_own, up_own, gate_other, up_other, down_own, down_other):
    _, rows, half = x.shape
    width = 2 * half
    ff_half = gate_own.shape[2]
    ff = 2 * ff_half
    tile = 256
    places = 2 * (ff_half // tile)
    anywhere = pl.BlockSpec(memory_space=pl.ANY)
    whole = pl.BlockSpec(memory_space=pltpu.VMEM)
    return pl.pallas_call(
        expert_kernel,
        out_shape=(
            jax.ShapeDtypeStruct((2, rows, half), jnp.bfloat16),
            jax.ShapeDtypeStruct((rows, ff), jnp.bfloat16),
            jax.ShapeDtypeStruct((8, 128), jnp.float32),
        ),
        in_specs=[pl.BlockSpec(memory_space=pltpu.SMEM)] + [anywhere] * 7,
        out_specs=(whole, whole, whole),
        scratch_shapes=[
            pltpu.VMEM((2, rows, half), jnp.bfloat16),
            pltpu.VMEM((places, 2, width, tile), jnp.bfloat16),
            pltpu.VMEM((2, ff, half), jnp.bfloat16),
            pltpu.SemaphoreType.DMA((2,)),
            pltpu.SemaphoreType.DMA((2 * places,)),
            pltpu.SemaphoreType.DMA((2,)),
        ],
        compiler_params=pltpu.CompilerParams(vmem_limit_bytes=48 * 1024 * 1024),
        cost_estimate=pl.CostEstimate(
            flops=2 * rows * width * ff * 3, bytes_accessed=6 * width * ff + 4 * rows * width,
            transcendentals=rows * ff,
        ),
    )(core, x, gate_own, up_own, gate_other, up_other, down_own, down_other)


def swap(array):
    return lax.ppermute(array, "token", [(0, 1), (1, 0)])


def shards(tokens, routes, mixing, gate_weight, up_weight, down_weight):
    tok_rows, half = tokens.shape
    experts = lax.axis_size("expert")
    capacity = 2 * tok_rows * routes.shape[1] // experts
    part = capacity // 2
    core = lax.axis_index("token")
    names = jnp.arange(experts, dtype=jnp.int32)
    match = routes.T[None, :, :] == names[:, None, None]
    chosen = jnp.any(match, axis=1)
    weight = jnp.sum(jnp.where(match, mixing.T[None], 0.0), axis=1)
    spots = jnp.arange(tok_rows, dtype=jnp.int32)
    before = (spots[:, None] < spots[None, :]).astype(jnp.bfloat16)
    rank = jnp.dot(chosen.astype(jnp.bfloat16), before, preferred_element_type=jnp.float32)
    key = jnp.where(chosen, rank.astype(jnp.int32), -1)
    counts = jnp.sum(chosen.astype(jnp.int32), axis=1)
    slot = jnp.arange(capacity, dtype=jnp.int32).reshape(2, 1, part)
    place = key[None, :, None, :] == slot[..., None]
    empty = (slot >= counts[None, :, None]).reshape(-1, 1)
    placing = place.astype(jnp.bfloat16).reshape(-1, tok_rows)
    mark = jnp.where(empty & (jnp.arange(half)[None, :] == 0), EMPTY, 0.0)
    outgoing = jnp.dot(placing, tokens, preferred_element_type=jnp.float32) + mark
    outgoing = outgoing.astype(jnp.bfloat16).reshape(2 * experts, part, half)
    received = lax.all_to_all(outgoing, ("token", "expert"), 0, 0, tiled=True)
    x = received.reshape(2, experts * part, half)
    gate_other, up_other, down_other = swap(gate_weight), swap(up_weight), swap(down_weight)
    out, hidden, count = run_experts(
        core.reshape(1), x, gate_weight, up_weight, gate_other, up_other, down_weight, down_other
    )
    returned = lax.all_to_all(
        out.reshape(2 * experts, part, half), ("token", "expert"), 0, 0, tiled=True
    ).reshape(-1, half)
    hidden_other, count_other = swap(hidden), swap(count)
    ff_half = gate_weight.shape[2]

    def outer(array):
        own = lax.dynamic_slice_in_dim(array, core * ff_half, ff_half, 1)
        return lax.dot_general(
            own, array, (((0,), (0,)), ((), ())), preferred_element_type=jnp.float32
        )

    total = count[0, 0] + count_other[0, 0]
    hessian = (2.0 / total * (outer(hidden) + outer(hidden_other)))[None]
    mixes = jnp.where(place, weight[None, :, None, :], 0.0).reshape(-1, tok_rows)
    high = lax.reduce_precision(mixes, 8, 7)
    mixes = jnp.concatenate([high, mixes - high], axis=1).astype(jnp.bfloat16)
    mixed = lax.dot_general(
        mixes, returned, (((0,), (0,)), ((), ())), preferred_element_type=jnp.float32
    )
    mixed = (mixed[:tok_rows] + mixed[tok_rows:]).astype(jnp.bfloat16)
    return mixed, hessian


def solution(mesh):
    placed = (
        P("expert", "token"),
        P("expert", None),
        P("expert", None),
        P("expert", None, "token"),
        P("expert", None, "token"),
        P("expert", None, "token"),
    )
    return jax.shard_map(
        shards,
        mesh=mesh,
        in_specs=placed,
        out_specs=(P("expert", "token"), P("expert", "token", None)),
        check_vma=False,
    )
```

time: 199 us -> 147 us (0.74); the launches traced: 199 us -> 145 us
  blocking collectives: 57.3 us -> 0 us
  Pallas kernels: 0 us -> 20.2 us
  waiting for transfers between devices: 66.9 us -> 84.4 us
  matrix products: 24.9 us -> 8.6 us
  between operations: 14.9 us -> 2.1 us
  local copies, waits for them, and re-layouts: 8.72 us -> 3.13 us
  starting transfers between devices: 21 us -> 24 us
  other arithmetic: 5.11 us -> 2.14 us
    all_to_all x1 -> x0, blocking collectives: 57.3 us -> none  [shards(): lax.all_to_all(outgoing, 'expert', split_axis=0, concat_axis=0, tiled=True)]
    all_to_all x2, waiting for transfers between devices: 43.5 us -> 83 us  [the longest x1 45.7 us: shards(): received = lax.all_to_all(outgoing, ('token', 'expert'), 0, 0, tiled=True)]
    all_gather x2 -> x0, waiting for transfers between devices: 23.4 us -> none  [the longest x1 19.5 us: shards(): piece = lax.all_gather(rows_in, 'token', axis=1, tiled=True)]
    pallas_call x0 -> x1, Pallas kernels: none -> 20.2 us  [run_experts(): pl.pallas_call(expert_kernel, out_shape=(jax.ShapeDtypeStruct((2, rows, h...]
    dot_general x5, matrix products: 24.9 us -> 8.6 us  [the longest x2 2.84 us: outer(): lax.dot_general(own, array, (((0,), (0,)), ((), ())), preferred_element_t...]
    gather x1 -> x0, local copies, waits for them, and re-layouts: 6.45 us -> none  [shards(): picked = returned.reshape(slot_total, feat_width)[target]]
    reduce_sum x4 -> x2, other arithmetic: 3.83 us -> 0.19 us  [the longest x1 0.11 us: shards(): counts = jnp.sum(chosen.astype(jnp.int32), axis=1)]
    ppermute x0 -> x5, starting transfers between devices: none -> 3.5 us  [swap(): return lax.ppermute(array, 'token', [(0, 1), (1, 0)])]
  transfers between devices with their start and end apart: 4 -> 7, of which waited for: 3 -> 3; matrix products, arithmetic and copies ran while one was open for 6% -> 6% of each run, Pallas kernels for 0% -> 0%
where the time goes in v1:
time: 147 us; the launch traced here: 145 us
  waiting for transfers between devices  84.4 us (57%)
  starting transfers between devices  24 us (16%)
  Pallas kernels  20.2 us (14%)
  matrix products  8.6 us (6%)
  local copies, waits for them, and re-layouts  3.13 us (2%)
  other arithmetic  2.14 us (1%)
  between operations  2.1 us (1%)
    all_to_all x1, waiting for transfers between devices, shards(): received = lax.all_to_all(outgoing, ('token', 'expert'), 0, 0, tiled=True)  45.7 us
    all_to_all x1, waiting for transfers between devices, shards(): lax.all_to_all(out.reshape(2 * experts, part, half), ('token', 'expert'),...  37.3 us
    pallas_call x1, Pallas kernels, run_experts(): pl.pallas_call(expert_kernel, out_shape=(jax.ShapeDtypeStruct((2, rows, h...  20.2 us
    all_to_all x1, starting transfers between devices, shards(): received = lax.all_to_all(outgoing, ('token', 'expert'), 0, 0, tiled=True)  10.6 us
    all_to_all x1, starting transfers between devices, shards(): lax.all_to_all(out.reshape(2 * experts, part, half), ('token', 'expert'),...  9.94 us
    ppermute x5, starting transfers between devices, swap(): return lax.ppermute(array, 'token', [(0, 1), (1, 0)])  3.5 us
  transfers between devices with their start and end apart: 7, of which 3 were waited for; matrix products, arithmetic and copies ran while one was open for 6% of the time, Pallas kernels for 0%

profile of v1, /device:TPU:1, one launch (start us, length us, event | category | flops | bytes accessed | tf_op | source)
XLA Modules:
  0.0 144.5 jit_solution(679744155028506092)
XLA Ops:
  0.6 0.0 copy-start
  0.6 1.5 %collective-permute-start = (bf16[1,3584,512]{2,1,0:T(8,128)(2,1)}, bf16[1,3584,512]{2,1,0:T(8,128)(2,1)}, u32[]{:S(2)}, u32[]{:S(2)}) collective-permute-start(bf16[1,3584,512]{2,1,0:T(8,128)(2,1)} %gate_own.1), channel_id=1, source_target_pairs={{0,1},{1,0},{2,3},{3,2},{4,5},{5,4},{6,7},{7,6},{8,9},{9,8},{10,11... | collective-permute-start | bytes 11010056 | tf_op jit(solution)/shard_map/ppermute | solution.py:108
  2.1 0.1 collective-permute-start.1
  2.2 0.4 collective-permute-start.2
  2.7 0.8 fusion.15
  3.4 0.1 fusion.3
  3.6 0.1 convert_reduce_fusion
  3.7 0.1 eq.55
  3.8 0.1 ge.17
  3.9 0.1 ge.18
  4.0 0.2 bitcast_compare_fusion
  4.2 2.8 %fusion.2 = bf16[128,8,1792]{2,1,0:T(8,128)(2,1)} fusion(pred[1792]{0:T(1024)(128)(4,1)S(1)} %iota_compare_fusion.3, pred[1024]{0:T(1024)(128)(4,1)S(1)} %ge.19, pred[1024,64]{1,0:T(32,128)(4,1)S(1)} %bitcast_compare_fusion, bf16[64,1792]{1,0:T(8,128)(2,1)S(1)} %copy-done), kind=kOutput, calls=%fused_computation.3 | convolution fusion | flops 242221056 | bytes 3967744 | tf_op jit(solution)/shard_map/dot_general | solution.py:131
  7.0 10.6 %all-to-all-start = ((bf16[128,8,1792]{2,1,0:T(8,128)(2,1)}), bf16[128,8,1792]{2,1,0:T(8,128)(2,1)}, u32[]{:S(2)}, u32[]{:S(2)}) async-start(bf16[128,8,1792]{2,1,0:T(8,128)(2,1)} %fusion.2), calls=%async_computation | async-start | bytes 7340032 | tf_op jit(solution)/shard_map/all_to_all | solution.py:133
  17.6 45.7 %all-to-all-done = bf16[128,8,1792]{2,1,0:T(8,128)(2,1)} async-done(((bf16[128,8,1792]{2,1,0:T(8,128)(2,1)}), bf16[128,8,1792]{2,1,0:T(8,128)(2,1)}, u32[]{:S(2)}, u32[]{:S(2)}) %all-to-all-start) | async-done | bytes 3670048 | tf_op jit(solution)/shard_map/all_to_all | solution.py:133
  63.3 0.0 collective-permute-done.gate_other
  63.3 0.0 collective-permute-done.1.up_other
  63.3 20.2 %shard_map.77 = (bf16[2,512,1792]{2,1,0:T(8,128)(2,1)S(1)}, bf16[512,1024]{1,0:T(8,128)(2,1)S(1)}, f32[8,128]{1,0:T(8,128)S(1)}) custom-call(s32[1]{0:T(128)} %bitcast.4.core_ref, bf16[2,512,1792]{2,1,0:T(8,128)(2,1)} %bitcast.6.x_hbm, bf16[1,3584,512]{2,1,0:T(8,128)(2,1)} %gate_own.1, bf16[1,3584,512]{2,1,0:T(8,128)(2,1)} %up_own.1, ...), custom_call_target="tpu_custom_call" | custom-call | flops 11274289152 | bytes 29360128 | tf_op jit(solution)/shard_map/pallas_call | solution.py:82
  83.5 1.8 %copy-done.1 = bf16[2,512,1792]{2,1,0:T(8,128)(2,1)} copy-done((bf16[2,512,1792]{2,1,0:T(8,128)(2,1)}, bf16[2,512,1792]{2,1,0:T(8,128)(2,1)S(1)}, u32[]{:S(2)}) %copy-start.1) | copy-done | bytes 3670040
  85.4 9.9 %all-to-all-start.1 = ((bf16[128,8,1792]{2,1,0:T(8,128)(2,1)}), bf16[128,8,1792]{2,1,0:T(8,128)(2,1)}, u32[]{:S(2)}, u32[]{:S(2)}) async-start(bf16[128,8,1792]{2,1,0:T(8,128)(2,1)} %bitcast.30), calls=%async_computation.1 | async-start | bytes 7340032 | tf_op jit(solution)/shard_map/all_to_all | solution.py:139
  95.3 1.4 collective-permute-start.4
  96.7 0.1 collective-permute-start.3
  96.8 0.1 select_reduce_fusion
  96.9 0.2 reduce-precision_convert_fusion
  97.1 0.5 slice.14
  97.6 1.4 collective-permute-done.3
  99.0 0.5 slice.15
  100.8 0.0 collective-permute-done.4
  100.8 0.8 fusion.5
  101.6 2.1 %multiply_bitcast_fusion = f32[1,512,1024]{2,1,0:T(8,128)} fusion(f32[512,1024]{1,0:T(8,128)S(1)} %fusion.5, f32[]{:T(128)} %bitcast.9, bf16[512,1024]{1,0:T(8,128)(2,1)S(1)} %get-tuple-element.7, s32[]{:T(128)S(6)} %select_n.25), kind=kOutput, calls=%fused_computation.4 | convolution fusion | flops 537919488 | bytes 5767176 | tf_op jit(solution)/shard_map/dot_general | solution.py:147
  103.7 37.3 %all-to-all-done.1 = bf16[128,8,1792]{2,1,0:T(8,128)(2,1)} async-done(((bf16[128,8,1792]{2,1,0:T(8,128)(2,1)}), bf16[128,8,1792]{2,1,0:T(8,128)(2,1)}, u32[]{:S(2)}, u32[]{:S(2)}) %all-to-all-start.1) | async-done | bytes 3670048 | tf_op jit(solution)/shard_map/all_to_all | solution.py:139
  141.0 2.8 %fusion = f32[128,1792]{1,0:T(8,128)S(1)} fusion(bf16[128,8,1792]{2,1,0:T(8,128)(2,1)} %all-to-all-done.1, bf16[1024,64]{1,0:T(8,128)(2,1)S(1)} %get-tuple-element.9, bf16[1024,64]{1,0:T(8,128)(2,1)S(1)} %get-tuple-element.8), kind=kOutput, calls=%fused_computation.1 | convolution fusion | flops 470286336 | bytes 4849664 | tf_op jit(solution)/shard_map/dot_general | solution.py:156
  143.8 0.7 fusion.11
  (11 shorter events, 0.0 us)
Async XLA Ops:
  0.6 3.6 %copy-start = (bf16[64,1792]{1,0:T(8,128)(2,1)S(1)}, bf16[64,1792]{1,0:T(8,128)(2,1)}, u32[]{:S(2)}) copy-start(bf16[64,1792]{1,0:T(8,128)(2,1)} %param.6) | copy-start | bytes 688132
  0.6 62.7 %collective-permute-start = (bf16[1,3584,512]{2,1,0:T(8,128)(2,1)}, bf16[1,3584,512]{2,1,0:T(8,128)(2,1)}, u32[]{:S(2)}, u32[]{:S(2)}) collective-permute-start(bf16[1,3584,512]{2,1,0:T(8,128)(2,1)} %gate_own.1), channel_id=1, source_target_pairs={{0,1},{1,0},{2,3},{3,2},{4,5},{5,4},{6,7},{7,6},{8,9},{9,8},{10,11... | collective-permute-start | bytes 11010056 | tf_op jit(solution)/shard_map/ppermute | solution.py:108
  2.1 61.2 %collective-permute-start.1 = (bf16[1,3584,512]{2,1,0:T(8,128)(2,1)}, bf16[1,3584,512]{2,1,0:T(8,128)(2,1)}, u32[]{:S(2)}, u32[]{:S(2)}) collective-permute-start(bf16[1,3584,512]{2,1,0:T(8,128)(2,1)} %up_own.1), channel_id=1, source_target_pairs={{0,1},{1,0},{2,3},{3,2},{4,5},{5,4},{6,7},{7,6},{8,9},{9,8},{10,11... | collective-permute-start | bytes 11010056 | tf_op jit(solution)/shard_map/ppermute | solution.py:108
  2.2 61.1 %collective-permute-start.2 = (bf16[1,1024,1792]{2,1,0:T(8,128)(2,1)}, bf16[1,1024,1792]{2,1,0:T(8,128)(2,1)}, u32[]{:S(2)}, u32[]{:S(2)}) collective-permute-start(bf16[1,1024,1792]{2,1,0:T(8,128)(2,1)} %down_own.1), channel_id=1, source_target_pairs={{0,1},{1,0},{2,3},{3,2},{4,5},{5,4},{6,7},{7,6},{8,9},{9,8},{10,11... | collective-permute-start | bytes 11010056 | tf_op jit(solution)/shard_map/ppermute | solution.py:108
  7.0 56.3 %all-to-all-start = ((bf16[128,8,1792]{2,1,0:T(8,128)(2,1)}), bf16[128,8,1792]{2,1,0:T(8,128)(2,1)}, u32[]{:S(2)}, u32[]{:S(2)}) async-start(bf16[128,8,1792]{2,1,0:T(8,128)(2,1)} %fusion.2), calls=%async_computation | async-start | bytes 7340032 | tf_op jit(solution)/shard_map/all_to_all | solution.py:133
  83.5 1.8 %copy-start.1 = (bf16[2,512,1792]{2,1,0:T(8,128)(2,1)}, bf16[2,512,1792]{2,1,0:T(8,128)(2,1)S(1)}, u32[]{:S(2)}) copy-start(bf16[2,512,1792]{2,1,0:T(8,128)(2,1)S(1)} %get-tuple-element.5) | copy-start | bytes 11010052
  85.3 11.4 %copy-start.2 = (s32[64,8]{0,1:T(8,128)S(1)}, s32[64,8]{0,1:T(8,128)}, u32[]{:S(2)}) copy-start(s32[64,8]{0,1:T(8,128)} %param.7) | copy-start | bytes 6148
  85.4 11.4 %copy-start.3 = (f32[64,8]{0,1:T(8,128)S(1)}, f32[64,8]{0,1:T(8,128)}, u32[]{:S(2)}) copy-start(f32[64,8]{0,1:T(8,128)} %param.8) | copy-start | bytes 6148
  85.4 55.6 %all-to-all-start.1 = ((bf16[128,8,1792]{2,1,0:T(8,128)(2,1)}), bf16[128,8,1792]{2,1,0:T(8,128)(2,1)}, u32[]{:S(2)}, u32[]{:S(2)}) async-start(bf16[128,8,1792]{2,1,0:T(8,128)(2,1)} %bitcast.30), calls=%async_computation.1 | async-start | bytes 7340032 | tf_op jit(solution)/shard_map/all_to_all | solution.py:139
  95.3 5.5 %collective-permute-start.4 = (bf16[512,1024]{1,0:T(8,128)(2,1)S(1)}, bf16[512,1024]{1,0:T(8,128)(2,1)S(1)}, u32[]{:S(2)}, u32[]{:S(2)}) collective-permute-start(bf16[512,1024]{1,0:T(8,128)(2,1)S(1)} %get-tuple-element.7), channel_id=1, source_target_pairs={{0,1},{1,0},{2,3},{3,2},{4,5},{5,4},{6,7},{7,6},{8,9},{9,8},{10,11... | collective-permute-start | bytes 3145736 | tf_op jit(solution)/shard_map/ppermute | solution.py:108
  96.7 2.3 %collective-permute-start.3 = (f32[8,128]{1,0:T(8,128)S(1)}, f32[8,128]{1,0:T(8,128)S(1)}, u32[]{:S(2)}, u32[]{:S(2)}) collective-permute-start(f32[8,128]{1,0:T(8,128)S(1)} %get-tuple-element.6), channel_id=1, source_target_pairs={{0,1},{1,0},{2,3},{3,2},{4,5},{5,4},{6,7},{7,6},{8,9},{9,8},{10,11... | collective-permute-start | bytes 12296 | tf_op jit(solution)/shard_map/ppermute | solution.py:108

commit v2 on v1

v2 whole, which is shorter than its diff:
```python
import functools

import jax
import jax.numpy as jnp
from jax import lax
from jax.experimental import pallas as pl
from jax.experimental.pallas import tpu as pltpu
from jax.sharding import PartitionSpec as P

EMPTY = 64.0
LOOKAHEAD = 4
VMEM_LIMIT = 61 * 1024 * 1024


def route_kernel(experts, part, wide, routes_ref, tokens_ref, out_hbm, out, sems):
    tok_rows, half = tokens_ref.shape
    steps = half // wide
    names = lax.broadcasted_iota(jnp.int32, (experts, tok_rows), 0)
    chosen = names == routes_ref[0:1, :]
    for k in range(1, routes_ref.shape[0]):
        chosen = chosen | (names == routes_ref[k : k + 1, :])
    first = lax.broadcasted_iota(jnp.int32, (tok_rows, tok_rows), 0)
    second = lax.broadcasted_iota(jnp.int32, (tok_rows, tok_rows), 1)
    rank = jnp.dot(
        chosen.astype(jnp.bfloat16), (first < second).astype(jnp.bfloat16),
        preferred_element_type=jnp.float32,
    )
    key = jnp.where(chosen, rank, -1.0)
    ones = jnp.ones((tok_rows, 128), jnp.bfloat16)
    rows = experts * part
    lane = lax.broadcasted_iota(jnp.int32, (rows, wide), 1)
    slot = lax.broadcasted_iota(jnp.int32, (experts, part, tok_rows), 1).astype(jnp.float32)
    copies = []
    for c in range(2):
        place = jnp.where(key[:, None, :] == slot + float(c * part), 1.0, 0.0)
        place = place.reshape(rows, tok_rows).astype(jnp.bfloat16)
        taken = jnp.dot(place, ones, preferred_element_type=jnp.float32)[:, :1]
        for n in range(steps):
            columns = pl.ds(n * wide, wide)
            picked = jnp.dot(place, tokens_ref[:, columns], preferred_element_type=jnp.float32)
            if n == 0:
                picked = picked + jnp.where(lane == 0, EMPTY * (1.0 - taken), 0.0)
            spot = pl.ds(c * rows, rows)
            out[spot, columns] = picked.astype(out.dtype)
            copy = pltpu.make_async_copy(
                out.at[spot, columns], out_hbm.at[spot, columns], sems.at[c * steps + n]
            )
            copy.start()
            copies.append(copy)
    for copy in copies:
        copy.wait()


def place_rows(routes, tokens, experts, part):
    tok_rows, half = tokens.shape
    shape = (2 * experts * part, half)
    wide = 256
    return pl.pallas_call(
        functools.partial(route_kernel, experts, part, wide),
        out_shape=jax.ShapeDtypeStruct(shape, jnp.bfloat16),
        in_specs=[pl.BlockSpec(memory_space=pltpu.VMEM)] * 2,
        out_specs=pl.BlockSpec(memory_space=pltpu.HBM),
        scratch_shapes=[
            pltpu.VMEM(shape, jnp.bfloat16), pltpu.SemaphoreType.DMA((2 * (half // wide),))
        ],
        compiler_params=pltpu.CompilerParams(vmem_limit_bytes=VMEM_LIMIT),
    )(routes, tokens)


def expert_kernel(
    core_ref, x_hbm, gate_own, up_own, gate_other, up_other, down_own, down_other,
    out_hbm, hid_ref, count_ref, x, first, second, outs, x_sems, f_sems, s_sems, o_sems,
):
    core = core_ref[0]
    half = x.shape[2]
    ff_half = gate_own.shape[2]
    wide = 256

    def load_x(f):
        return pltpu.make_async_copy(x_hbm.at[f], x.at[f], x_sems.at[f])

    def load_first(i, src, f):
        return pltpu.make_async_copy(
            src.at[0, pl.ds(f * half, half)], first.at[i, f], f_sems.at[2 * i + f]
        )

    queue = []
    cut = 768
    for i, src in enumerate((gate_own, up_own, gate_other, up_other)):
        for f in range(2):
            if i == 0 and f == 0:
                for n, span in enumerate((pl.ds(0, cut), pl.ds(cut, half - cut))):
                    queue.append(
                        pltpu.make_async_copy(
                            x_hbm.at[0, :, span], x.at[0, :, span], x_sems.at[2 * n]
                        )
                    )
                    queue.append(
                        pltpu.make_async_copy(
                            src.at[0, span], first.at[0, 0, span], f_sems.at[8 * n]
                        )
                    )
                continue
            if i == 0:
                queue.append(load_x(f))
            queue.append(load_first(i, src, f))
    for i, src in enumerate((down_own, down_other)):
        queue.append(pltpu.make_async_copy(src.at[0], second.at[i], s_sems.at[i]))
    started = []

    def ahead(count):
        while len(started) < min(count, len(queue)):
            copy = queue[len(started)]
            copy.start()
            started.append(copy)

    done = []

    def ready(count):
        while len(done) < count:
            queue[len(done)].wait()
            done.append(None)
            ahead(len(done) + LOOKAHEAD)

    ahead(LOOKAHEAD)

    def product(i):
        if i == 0:
            ready(2)
            total = jnp.dot(x[0, :, :cut], first[0, 0, :cut], preferred_element_type=jnp.float32)
            ready(4)
            total = total + jnp.dot(x[0, :, cut:], first[0, 0, cut:], preferred_element_type=jnp.float32)
        else:
            ready(5 + 2 * i)
            total = jnp.dot(x[0], first[i, 0], preferred_element_type=jnp.float32)
        ready(6 + 2 * i)
        return total + jnp.dot(x[1], first[i, 1], preferred_element_type=jnp.float32)

    for side in range(2):
        gate = product(2 * side)
        if side == 0:
            valid = x[0, :, :128].astype(jnp.float32)[:, :1] < EMPTY / 2
            count_ref[...] = jnp.full(count_ref.shape, jnp.sum(valid.astype(jnp.float32)))
        upper = product(2 * side + 1)
        hidden = jnp.where(valid, gate / (1.0 + jnp.exp(-gate)) * upper, 0.0)
        base = (core if side == 0 else 1 - core) * ff_half
        hid_ref[:, pl.ds(pl.multiple_of(base, ff_half), ff_half)] = hidden.astype(hid_ref.dtype)
    copies = []
    for side in range(2):
        ready(13 + side)
        target = core if side == 0 else 1 - core
        for n in range(half // wide):
            columns = pl.ds(n * wide, wide)
            outs[side, :, columns] = jnp.dot(
                hid_ref[...], second[side, :, columns], preferred_element_type=jnp.float32
            ).astype(outs.dtype)
            copy = pltpu.make_async_copy(
                outs.at[side, :, columns], out_hbm.at[target, :, columns],
                o_sems.at[side * (half // wide) + n],
            )
            copy.start()
            copies.append(copy)
    for copy in copies:
        copy.wait()


def run_experts(core, x, gate_own, up_own, gate_other, up_other, down_own, down_other):
    _, rows, half = x.shape
    width = 2 * half
    ff_half = gate_own.shape[2]
    ff = 2 * ff_half
    whole = pl.BlockSpec(memory_space=pltpu.VMEM)
    far = pl.BlockSpec(memory_space=pltpu.HBM)
    return pl.pallas_call(
        expert_kernel,
        out_shape=(
            jax.ShapeDtypeStruct((2, rows, half), jnp.bfloat16),
            jax.ShapeDtypeStruct((rows, ff), jnp.bfloat16),
            jax.ShapeDtypeStruct((8, 128), jnp.float32),
        ),
        in_specs=[pl.BlockSpec(memory_space=pltpu.SMEM)] + [far] * 7,
        out_specs=(far, whole, whole),
        scratch_shapes=[
            pltpu.VMEM((2, rows, half), jnp.bfloat16),
            pltpu.VMEM((4, 2, half, ff_half), jnp.bfloat16),
            pltpu.VMEM((2, ff, half), jnp.bfloat16),
            pltpu.VMEM((2, rows, half), jnp.bfloat16),
            pltpu.SemaphoreType.DMA((3,)),
            pltpu.SemaphoreType.DMA((9,)),
            pltpu.SemaphoreType.DMA((2,)),
            pltpu.SemaphoreType.DMA((2 * (half // 256),)),
        ],
        compiler_params=pltpu.CompilerParams(vmem_limit_bytes=VMEM_LIMIT),
        cost_estimate=pl.CostEstimate(
            flops=2 * rows * width * ff * 3, bytes_accessed=6 * width * ff + 4 * rows * width,
            transcendentals=rows * ff,
        ),
    )(core, x, gate_own, up_own, gate_other, up_other, down_own, down_other)


def mix_kernel(mixes_ref, returned_hbm, out_ref, returned, sems):
    tok_rows = out_ref.shape[0]
    parts, rows, _ = returned.shape
    copies = []
    for n in range(parts):
        span = pl.ds(n * rows, rows)
        copies.append(pltpu.make_async_copy(returned_hbm.at[span], returned.at[n], sems.at[n]))
        copies[-1].start()
    total = None
    for n, copy in enumerate(copies):
        copy.wait()
        both = jnp.dot(
            mixes_ref[:, n * rows : (n + 1) * rows], returned[n], preferred_element_type=jnp.float32
        )
        total = both if total is None else total + both
    out_ref[...] = (total[:tok_rows] + total[tok_rows:]).astype(out_ref.dtype)


def mix_rows(mixes, returned):
    rows, half = returned.shape
    parts = 4
    return pl.pallas_call(
        mix_kernel,
        out_shape=jax.ShapeDtypeStruct((mixes.shape[0] // 2, half), jnp.bfloat16),
        in_specs=[pl.BlockSpec(memory_space=pltpu.VMEM), pl.BlockSpec(memory_space=pltpu.HBM)],
        out_specs=pl.BlockSpec(memory_space=pltpu.VMEM),
        scratch_shapes=[
            pltpu.VMEM((parts, rows // parts, half), jnp.bfloat16),
            pltpu.SemaphoreType.DMA((parts,)),
        ],
        compiler_params=pltpu.CompilerParams(vmem_limit_bytes=VMEM_LIMIT),
    )(mixes, returned)


def swap(array):
    return lax.ppermute(array, "token", [(0, 1), (1, 0)])


def mix_table(routes, mixing, experts, part):
    tok_rows = routes.shape[0]
    names = jnp.arange(experts, dtype=jnp.int32)
    match = routes[:, :, None] == names[None, None, :]
    chosen = jnp.any(match, axis=1)
    weight = jnp.sum(jnp.where(match, mixing[:, :, None], 0.0), axis=1)
    spots = jnp.arange(tok_rows, dtype=jnp.int32)
    before = (spots[:, None] > spots[None, :]).astype(jnp.bfloat16)
    rank = jnp.dot(before, chosen.astype(jnp.bfloat16), preferred_element_type=jnp.float32)
    key = jnp.where(chosen, rank.astype(jnp.int32), -1)
    slot = jnp.arange(2 * part, dtype=jnp.int32).reshape(2, 1, part)
    place = key[:, None, :, None] == slot[None]
    mixes = jnp.where(place, weight[:, None, :, None], 0.0).reshape(tok_rows, -1)
    high = lax.reduce_precision(mixes, 8, 7)
    return jnp.concatenate([high, mixes - high], axis=0).astype(jnp.bfloat16)


def shards(tokens, routes, mixing, gate_weight, up_weight, down_weight):
    tok_rows, half = tokens.shape
    experts = lax.axis_size("expert")
    capacity = 2 * tok_rows * routes.shape[1] // experts
    part = capacity // 2
    core = lax.axis_index("token")
    outgoing = place_rows(routes.T, tokens, experts, part).reshape(2 * experts, part, half)
    received = lax.all_to_all(outgoing, ("token", "expert"), 0, 0, tiled=True)
    x = received.reshape(2, experts * part, half)
    _, gate_sent, up_sent, down_sent = lax.optimization_barrier(
        (outgoing, gate_weight, up_weight, down_weight)
    )
    gate_other, up_other, down_other = swap(gate_sent), swap(up_sent), swap(down_sent)
    out, hidden, count = run_experts(
        core.reshape(1), x, gate_weight, up_weight, gate_other, up_other, down_weight, down_other
    )
    returned = lax.all_to_all(
        out.reshape(2 * experts, part, half), ("token", "expert"), 0, 0, tiled=True
    ).reshape(-1, half)
    hidden_other, count_other = swap(hidden), swap(count)
    ff_half = gate_weight.shape[2]

    def outer(array):
        own = lax.dynamic_slice_in_dim(array, core * ff_half, ff_half, 1)
        return lax.dot_general(
            own, array, (((0,), (0,)), ((), ())), preferred_element_type=jnp.float32
        )

    total = count[0, 0] + count_other[0, 0]
    hessian = (2.0 / total * (outer(hidden) + outer(hidden_other)))[None]
    mixed = mix_rows(mix_table(routes, mixing, experts, part), returned)
    return mixed, hessian


def solution(mesh):
    placed = (
        P("expert", "token"),
        P("expert", None),
        P("expert", None),
        P("expert", None, "token"),
        P("expert", None, "token"),
        P("expert", None, "token"),
    )
    return jax.shard_map(
        shards,
        mesh=mesh,
        in_specs=placed,
        out_specs=(P("expert", "token"), P("expert", "token", None)),
        check_vma=False,
    )
```

time: 147 us -> 143 us (0.973)
  matrix products: 8.6 us -> 2.98 us
  Pallas kernels: 20.2 us -> 25.6 us
  waiting for transfers between devices: 84.4 us -> 82.6 us
    pallas_call x0 -> x2, Pallas kernels: none -> 7.39 us  [the longest x1 3.99 us: mix_rows(): pl.pallas_call(mix_kernel, out_shape=jax.ShapeDtypeStruct((mixes.shape[0]...]
    dot_general x3 -> x1, matrix products: 5.76 us -> 0.13 us  [mix_table(): jnp.dot(before, chosen.astype(jnp.bfloat16), preferred_element_type=jnp.f...]
    pallas_call x1, Pallas kernels: 20.2 us -> 18.2 us  [run_experts(): pl.pallas_call(expert_kernel, out_shape=(jax.ShapeDtypeStruct((2, rows, h...]
    unnamed x8 -> x10, local copies, waits for them, and re-layouts: 1.84 us -> 0.19 us
  transfers between devices with their start and end apart: 7 -> 7, of which waited for: 3 -> 2; matrix products, arithmetic and copies ran while one was open for 6% -> 4% of each run, Pallas kernels for 0% -> 0%
where the time goes in v2:
time: 143 us; the launch traced here: 140 us
  waiting for transfers between devices  82.6 us (58%)
  Pallas kernels  25.6 us (18%)
  starting transfers between devices  23.9 us (17%)
  matrix products  2.98 us (2%)
  between operations  2.3 us (2%)
  local copies, waits for them, and re-layouts  1.91 us (1%)
    all_to_all x1, waiting for transfers between devices, shards(): received = lax.all_to_all(outgoing, ('token', 'expert'), 0, 0, tiled=True)  45.7 us
    all_to_all x1, waiting for transfers between devices, shards(): lax.all_to_all(out.reshape(2 * experts, part, half), ('token', 'expert'),...  36.9 us
    pallas_call x1, Pallas kernels, run_experts(): pl.pallas_call(expert_kernel, out_shape=(jax.ShapeDtypeStruct((2, rows, h...  18.2 us
    all_to_all x1, starting transfers between devices, shards(): received = lax.all_to_all(outgoing, ('token', 'expert'), 0, 0, tiled=True)  10.6 us
    all_to_all x1, starting transfers between devices, shards(): lax.all_to_all(out.reshape(2 * experts, part, half), ('token', 'expert'),...  9.94 us
    pallas_call x1, Pallas kernels, mix_rows(): pl.pallas_call(mix_kernel, out_shape=jax.ShapeDtypeStruct((mixes.shape[0]...  3.99 us
    pallas_call x1, Pallas kernels, place_rows(): pl.pallas_call(functools.partial(route_kernel, experts, part, wide), out_...  3.4 us
    ppermute x5, starting transfers between devices, swap(): return lax.ppermute(array, 'token', [(0, 1), (1, 0)])  3.32 us
  transfers between devices with their start and end apart: 7, of which 2 were waited for; matrix products, arithmetic and copies ran while one was open for 4% of the time, Pallas kernels for 0%

profile of v2, /device:TPU:1, one launch (start us, length us, event | category | flops | bytes accessed | tf_op | source)
XLA Modules:
  0.0 140.4 jit_solution(11402415542185732751)
XLA Ops:
  0.6 3.4 %shard_map.77 = bf16[1024,1792]{1,0:T(8,128)(2,1)} custom-call(s32[8,64]{1,0:T(8,128)} %bitcast.18, bf16[64,1792]{1,0:T(8,128)(2,1)} %tokens_ref.1), custom_call_target="tpu_custom_call" | custom-call | tf_op jit(solution)/shard_map/pallas_call | solution.py:58
  4.0 1.5 %collective-permute-start = (bf16[1,3584,512]{2,1,0:T(8,128)(2,1)}, bf16[1,3584,512]{2,1,0:T(8,128)(2,1)}, u32[]{:S(2)}, u32[]{:S(2)}) collective-permute-start(bf16[1,3584,512]{2,1,0:T(8,128)(2,1)} %gate_own.1), channel_id=1, source_target_pairs={{0,1},{1,0},{2,3},{3,2},{4,5},{5,4},{6,7},{7,6},{8,9},{9,8},{10,11... | collective-permute-start | bytes 11010056 | tf_op jit(solution)/shard_map/ppermute | solution.py:236
  5.5 0.1 collective-permute-start.1
  5.6 0.4 collective-permute-start.2
  6.1 10.6 %all-to-all-start = ((bf16[128,8,1792]{2,1,0:T(8,128)(2,1)}), bf16[128,8,1792]{2,1,0:T(8,128)(2,1)}, u32[]{:S(2)}, u32[]{:S(2)}) async-start(bf16[128,8,1792]{2,1,0:T(8,128)(2,1)} %bitcast.14), calls=%async_computation | async-start | bytes 7340032 | tf_op jit(solution)/shard_map/all_to_all | solution.py:263
  16.7 45.7 %all-to-all-done = bf16[128,8,1792]{2,1,0:T(8,128)(2,1)} async-done(((bf16[128,8,1792]{2,1,0:T(8,128)(2,1)}), bf16[128,8,1792]{2,1,0:T(8,128)(2,1)}, u32[]{:S(2)}, u32[]{:S(2)}) %all-to-all-start) | async-done | bytes 3670048 | tf_op jit(solution)/shard_map/all_to_all | solution.py:263
  62.4 18.2 %shard_map.78 = (bf16[2,512,1792]{2,1,0:T(8,128)(2,1)}, bf16[512,1024]{1,0:T(8,128)(2,1)}, f32[8,128]{1,0:T(8,128)}) custom-call(s32[1]{0:T(128)} %bitcast.2.core_ref, bf16[2,512,1792]{2,1,0:T(8,128)(2,1)} %bitcast.5.x_hbm, bf16[1,3584,512]{2,1,0:T(8,128)(2,1)} %gate_own.1, bf16[1,3584,512]{2,1,0:T(8,128)(2,1)} %up_own.1, ...), custom_call_target="tpu_custom_call" | custom-call | flops 11274289152 | bytes 29360128 | tf_op jit(solution)/shard_map/pallas_call | solution.py:174
  80.5 0.0 copy-start
  80.5 0.0 copy-start.1
  80.6 0.0 copy-start.2
  80.6 9.9 %all-to-all-start.1 = ((bf16[128,8,1792]{2,1,0:T(8,128)(2,1)}), bf16[128,8,1792]{2,1,0:T(8,128)(2,1)}, u32[]{:S(2)}, u32[]{:S(2)}) async-start(bf16[128,8,1792]{2,1,0:T(8,128)(2,1)} %bitcast.15), calls=%async_computation.1 | async-start | bytes 7340032 | tf_op jit(solution)/shard_map/all_to_all | solution.py:272
  90.5 0.0 copy-start.3
  90.5 1.2 collective-permute-start.4
  91.8 0.1 copy.15
  91.8 0.1 copy.18
  91.9 0.2 select_reduce_fusion
  92.1 0.1 copy.19
  92.3 0.2 copy.20
  92.5 0.2 fusion.8
  92.6 0.1 fusion
  92.8 0.1 copy.16
  92.9 0.2 copy.17
  93.1 0.1 eq.39
  93.2 0.1 reduce-precision_convert_fusion
  93.3 0.1 collective-permute-start.3
  93.4 0.7 pad_maximum_fusion.mixes_ref
  94.1 0.5 slice.6
  94.6 0.5 slice.7
  96.5 0.8 fusion.1
  97.2 2.1 %multiply_bitcast_fusion = f32[1,512,1024]{2,1,0:T(8,128)} fusion(f32[512,1024]{1,0:T(8,128)S(1)} %fusion.1, f32[]{:T(128)} %bitcast.8, bf16[512,1024]{1,0:T(8,128)(2,1)S(1)} %copy-done, s32[]{:T(128)S(6)} %select_n.20), kind=kOutput, calls=%fused_computation | convolution fusion | flops 537919488 | bytes 5767176 | tf_op jit(solution)/shard_map/dot_general | solution.py:280
  99.3 36.9 %all-to-all-done.1 = bf16[128,8,1792]{2,1,0:T(8,128)(2,1)} async-done(((bf16[128,8,1792]{2,1,0:T(8,128)(2,1)}), bf16[128,8,1792]{2,1,0:T(8,128)(2,1)}, u32[]{:S(2)}, u32[]{:S(2)}) %all-to-all-start.1) | async-done | bytes 3670048 | tf_op jit(solution)/shard_map/all_to_all | solution.py:272
  136.2 4.0 %shard_map.79 = bf16[64,1792]{1,0:T(8,128)(2,1)} custom-call(bf16[128,1024]{1,0:T(8,128)(2,1)} %pad_maximum_fusion.mixes_ref, bf16[1024,1792]{1,0:T(8,128)(2,1)} %bitcast.7.returned_hbm), custom_call_target="tpu_custom_call" | custom-call | tf_op jit(solution)/shard_map/pallas_call | solution.py:222
  (13 shorter events, 0.1 us)
Async XLA Ops:
  4.0 58.3 %collective-permute-start = (bf16[1,3584,512]{2,1,0:T(8,128)(2,1)}, bf16[1,3584,512]{2,1,0:T(8,128)(2,1)}, u32[]{:S(2)}, u32[]{:S(2)}) collective-permute-start(bf16[1,3584,512]{2,1,0:T(8,128)(2,1)} %gate_own.1), channel_id=1, source_target_pairs={{0,1},{1,0},{2,3},{3,2},{4,5},{5,4},{6,7},{7,6},{8,9},{9,8},{10,11... | collective-permute-start | bytes 11010056 | tf_op jit(solution)/shard_map/ppermute | solution.py:236
  5.5 56.8 %collective-permute-start.1 = (bf16[1,3584,512]{2,1,0:T(8,128)(2,1)}, bf16[1,3584,512]{2,1,0:T(8,128)(2,1)}, u32[]{:S(2)}, u32[]{:S(2)}) collective-permute-start(bf16[1,3584,512]{2,1,0:T(8,128)(2,1)} %up_own.1), channel_id=1, source_target_pairs={{0,1},{1,0},{2,3},{3,2},{4,5},{5,4},{6,7},{7,6},{8,9},{9,8},{10,11... | collective-permute-start | bytes 11010056 | tf_op jit(solution)/shard_map/ppermute | solution.py:236
  5.6 56.7 %collective-permute-start.2 = (bf16[1,1024,1792]{2,1,0:T(8,128)(2,1)}, bf16[1,1024,1792]{2,1,0:T(8,128)(2,1)}, u32[]{:S(2)}, u32[]{:S(2)}) collective-permute-start(bf16[1,1024,1792]{2,1,0:T(8,128)(2,1)} %down_own.1), channel_id=1, source_target_pairs={{0,1},{1,0},{2,3},{3,2},{4,5},{5,4},{6,7},{7,6},{8,9},{9,8},{10,11... | collective-permute-start | bytes 11010056 | tf_op jit(solution)/shard_map/ppermute | solution.py:236
  6.1 56.3 %all-to-all-start = ((bf16[128,8,1792]{2,1,0:T(8,128)(2,1)}), bf16[128,8,1792]{2,1,0:T(8,128)(2,1)}, u32[]{:S(2)}, u32[]{:S(2)}) async-start(bf16[128,8,1792]{2,1,0:T(8,128)(2,1)} %bitcast.14), calls=%async_computation | async-start | bytes 7340032 | tf_op jit(solution)/shard_map/all_to_all | solution.py:263
  80.5 10.0 %copy-start = (bf16[512,1024]{1,0:T(8,128)(2,1)S(1)}, bf16[512,1024]{1,0:T(8,128)(2,1)}, u32[]{:S(2)}) copy-start(bf16[512,1024]{1,0:T(8,128)(2,1)} %get-tuple-element.13) | copy-start | bytes 3145732
  80.5 11.2 %copy-start.1 = (s32[64,8]{0,1:T(8,128)S(1)}, s32[64,8]{0,1:T(8,128)}, u32[]{:S(2)}) copy-start(s32[64,8]{0,1:T(8,128)} %param.7) | copy-start | bytes 6148
  80.6 11.3 %copy-start.2 = (f32[64,8]{0,1:T(8,128)S(1)}, f32[64,8]{0,1:T(8,128)}, u32[]{:S(2)}) copy-start(f32[64,8]{0,1:T(8,128)} %param.8) | copy-start | bytes 6148
  80.6 55.6 %all-to-all-start.1 = ((bf16[128,8,1792]{2,1,0:T(8,128)(2,1)}), bf16[128,8,1792]{2,1,0:T(8,128)(2,1)}, u32[]{:S(2)}, u32[]{:S(2)}) async-start(bf16[128,8,1792]{2,1,0:T(8,128)(2,1)} %bitcast.15), calls=%async_computation.1 | async-start | bytes 7340032 | tf_op jit(solution)/shard_map/all_to_all | solution.py:272
  90.5 2.7 %copy-start.3 = (f32[8,128]{1,0:T(8,128)S(1)}, f32[8,128]{1,0:T(8,128)}, u32[]{:S(2)}) copy-start(f32[8,128]{1,0:T(8,128)} %get-tuple-element.12) | copy-start | bytes 12292
  90.5 5.9 %collective-permute-start.4 = (bf16[512,1024]{1,0:T(8,128)(2,1)S(1)}, bf16[512,1024]{1,0:T(8,128)(2,1)S(1)}, u32[]{:S(2)}, u32[]{:S(2)}) collective-permute-start(bf16[512,1024]{1,0:T(8,128)(2,1)S(1)} %copy-done), channel_id=1, source_target_pairs={{0,1},{1,0},{2,3},{3,2},{4,5},{5,4},{6,7},{7,6},{8,9},{9,8},{10,11... | collective-permute-start | bytes 3145736 | tf_op jit(solution)/shard_map/ppermute | solution.py:236
  93.3 1.3 collective-permute-start.3

commit v3 on v2

--- a/solution.py
+++ b/solution.py
@@ -27,12 +27,13 @@
     )
     key = jnp.where(chosen, rank, -1.0)
     ones = jnp.ones((tok_rows, 128), jnp.bfloat16)
-    rows = experts * part
+    group = experts // 2
+    rows = group * 2 * part
     lane = lax.broadcasted_iota(jnp.int32, (rows, wide), 1)
-    slot = lax.broadcasted_iota(jnp.int32, (experts, part, tok_rows), 1).astype(jnp.float32)
+    slot = lax.broadcasted_iota(jnp.int32, (group, 2 * part, tok_rows), 1).astype(jnp.float32)
     copies = []
     for c in range(2):
-        place = jnp.where(key[:, None, :] == slot + float(c * part), 1.0, 0.0)
+        place = jnp.where(key[c * group : (c + 1) * group, None, :] == slot, 1.0, 0.0)
         place = place.reshape(rows, tok_rows).astype(jnp.bfloat16)
         taken = jnp.dot(place, ones, preferred_element_type=jnp.float32)[:, :1]
         for n in range(steps):
@@ -72,12 +73,13 @@
     out_hbm, hid_ref, count_ref, x, first, second, outs, x_sems, f_sems, s_sems, o_sems,
 ):
     core = core_ref[0]
-    half = x.shape[2]
+    _, groups, part, half = x.shape
+    rows = groups * part
     ff_half = gate_own.shape[2]
     wide = 256
 
     def load_x(f):
-        return pltpu.make_async_copy(x_hbm.at[f], x.at[f], x_sems.at[f])
+        return pltpu.make_async_copy(x_hbm.at[:, f], x.at[f], x_sems.at[f])
 
     def load_first(i, src, f):
         return pltpu.make_async_copy(
@@ -92,7 +94,7 @@
                 for n, span in enumerate((pl.ds(0, cut), pl.ds(cut, half - cut))):
                     queue.append(
                         pltpu.make_async_copy(
-                            x_hbm.at[0, :, span], x.at[0, :, span], x_sems.at[2 * n]
+                            x_hbm.at[:, 0, :, span], x.at[0, :, :, span], x_sems.at[2 * n]
                         )
                     )
                     queue.append(
@@ -127,19 +129,19 @@
     def product(i):
         if i == 0:
             ready(2)
-            total = jnp.dot(x[0, :, :cut], first[0, 0, :cut], preferred_element_type=jnp.float32)
+            total = jnp.dot(x[0, :, :, :cut].reshape(rows, cut), first[0, 0, :cut], preferred_element_type=jnp.float32)
             ready(4)
-            total = total + jnp.dot(x[0, :, cut:], first[0, 0, cut:], preferred_element_type=jnp.float32)
+            total = total + jnp.dot(x[0, :, :, cut:].reshape(rows, half - cut), first[0, 0, cut:], preferred_element_type=jnp.float32)
         else:
             ready(5 + 2 * i)
-            total = jnp.dot(x[0], first[i, 0], preferred_element_type=jnp.float32)
+            total = jnp.dot(x[0].reshape(rows, half), first[i, 0], preferred_element_type=jnp.float32)
         ready(6 + 2 * i)
-        return total + jnp.dot(x[1], first[i, 1], preferred_element_type=jnp.float32)
+        return total + jnp.dot(x[1].reshape(rows, half), first[i, 1], preferred_element_type=jnp.float32)
 
     for side in range(2):
         gate = product(2 * side)
         if side == 0:
-            valid = x[0, :, :128].astype(jnp.float32)[:, :1] < EMPTY / 2
+            valid = x[0, :, :, :128].astype(jnp.float32).reshape(rows, 128)[:, :1] < EMPTY / 2
             count_ref[...] = jnp.full(count_ref.shape, jnp.sum(valid.astype(jnp.float32)))
         upper = product(2 * side + 1)
         hidden = jnp.where(valid, gate / (1.0 + jnp.exp(-gate)) * upper, 0.0)
@@ -151,11 +153,12 @@
         target = core if side == 0 else 1 - core
         for n in range(half // wide):
             columns = pl.ds(n * wide, wide)
-            outs[side, :, columns] = jnp.dot(
+            result = jnp.dot(
                 hid_ref[...], second[side, :, columns], preferred_element_type=jnp.float32
-            ).astype(outs.dtype)
+            )
+            outs[side, :, :, columns] = result.reshape(groups, part, wide).astype(outs.dtype)
             copy = pltpu.make_async_copy(
-                outs.at[side, :, columns], out_hbm.at[target, :, columns],
+                outs.at[side, :, :, columns], out_hbm.at[:, target, :, columns],
                 o_sems.at[side * (half // wide) + n],
             )
             copy.start()
@@ -165,7 +168,8 @@
 
 
 def run_experts(core, x, gate_own, up_own, gate_other, up_other, down_own, down_other):
-    _, rows, half = x.shape
+    groups, _, part, half = x.shape
+    rows = groups * part
     width = 2 * half
     ff_half = gate_own.shape[2]
     ff = 2 * ff_half
@@ -174,17 +178,17 @@
     return pl.pallas_call(
         expert_kernel,
         out_shape=(
-            jax.ShapeDtypeStruct((2, rows, half), jnp.bfloat16),
+            jax.ShapeDtypeStruct((groups, 2, part, half), jnp.bfloat16),
             jax.ShapeDtypeStruct((rows, ff), jnp.bfloat16),
             jax.ShapeDtypeStruct((8, 128), jnp.float32),
         ),
         in_specs=[pl.BlockSpec(memory_space=pltpu.SMEM)] + [far] * 7,
         out_specs=(far, whole, whole),
         scratch_shapes=[
-            pltpu.VMEM((2, rows, half), jnp.bfloat16),
+            pltpu.VMEM((2, groups, part, half), jnp.bfloat16),
             pltpu.VMEM((4, 2, half, ff_half), jnp.bfloat16),
             pltpu.VMEM((2, ff, half), jnp.bfloat16),
-            pltpu.VMEM((2, rows, half), jnp.bfloat16),
+            pltpu.VMEM((2, groups, part, half), jnp.bfloat16),
             pltpu.SemaphoreType.DMA((3,)),
             pltpu.SemaphoreType.DMA((9,)),
             pltpu.SemaphoreType.DMA((2,)),
@@ -246,9 +250,9 @@
     before = (spots[:, None] > spots[None, :]).astype(jnp.bfloat16)
     rank = jnp.dot(before, chosen.astype(jnp.bfloat16), preferred_element_type=jnp.float32)
     key = jnp.where(chosen, rank.astype(jnp.int32), -1)
-    slot = jnp.arange(2 * part, dtype=jnp.int32).reshape(2, 1, part)
-    place = key[:, None, :, None] == slot[None]
-    mixes = jnp.where(place, weight[:, None, :, None], 0.0).reshape(tok_rows, -1)
+    slot = jnp.arange(2 * part, dtype=jnp.int32)
+    place = key[:, :, None] == slot
+    mixes = jnp.where(place, weight[:, :, None], 0.0).reshape(tok_rows, -1)
     high = lax.reduce_precision(mixes, 8, 7)
     return jnp.concatenate([high, mixes - high], axis=0).astype(jnp.bfloat16)
 
@@ -260,8 +264,8 @@
     part = capacity // 2
     core = lax.axis_index("token")
     outgoing = place_rows(routes.T, tokens, experts, part).reshape(2 * experts, part, half)
-    received = lax.all_to_all(outgoing, ("token", "expert"), 0, 0, tiled=True)
-    x = received.reshape(2, experts * part, half)
+    received = lax.all_to_all(outgoing, ("expert", "token"), 0, 0, tiled=True)
+    x = received.reshape(experts, 2, part, half)
     _, gate_sent, up_sent, down_sent = lax.optimization_barrier(
         (outgoing, gate_weight, up_weight, down_weight)
     )
@@ -270,7 +274,7 @@
         core.reshape(1), x, gate_weight, up_weight, gate_other, up_other, down_weight, down_other
     )
     returned = lax.all_to_all(
-        out.reshape(2 * experts, part, half), ("token", "expert"), 0, 0, tiled=True
+        out.reshape(2 * experts, part, half), ("expert", "token"), 0, 0, tiled=True
     ).reshape(-1, half)
     hidden_other, count_other = swap(hidden), swap(count)
     ff_half = gate_weight.shape[2]

time: 143 us -> 139 us (0.972); the launches traced: 140 us -> 139 us
  starting transfers between devices: 23.9 us -> 19.8 us
  waiting for transfers between devices: 82.6 us -> 85.5 us
    all_to_all x2, starting transfers between devices: 20.5 us -> 16.3 us  [the longest x1 10.6 us: shards(): received = lax.all_to_all(outgoing, ('expert', 'token'), 0, 0, tiled=True)]
    all_to_all x2, waiting for transfers between devices: 82.6 us -> 85.5 us  [the longest x1 47.1 us: shards(): received = lax.all_to_all(outgoing, ('expert', 'token'), 0, 0, tiled=True)]
where the time goes in v3:
time: 139 us
  waiting for transfers between devices  85.5 us (62%)
  Pallas kernels  25.5 us (18%)
  starting transfers between devices  19.8 us (14%)
  matrix products  2.97 us (2%)
  between operations  2.29 us (2%)
  local copies, waits for them, and re-layouts  1.89 us (1%)
    all_to_all x1, waiting for transfers between devices, shards(): received = lax.all_to_all(outgoing, ('expert', 'token'), 0, 0, tiled=True)  47.1 us
    all_to_all x1, waiting for transfers between devices, shards(): lax.all_to_all(out.reshape(2 * experts, part, half), ('expert', 'token'),...  38.4 us
    pallas_call x1, Pallas kernels, run_experts(): pl.pallas_call(expert_kernel, out_shape=(jax.ShapeDtypeStruct((groups, 2,...  18.2 us
    all_to_all x1, starting transfers between devices, shards(): received = lax.all_to_all(outgoing, ('expert', 'token'), 0, 0, tiled=True)  10.6 us
    all_to_all x1, starting transfers between devices, shards(): lax.all_to_all(out.reshape(2 * experts, part, half), ('expert', 'token'),...  5.69 us
    pallas_call x1, Pallas kernels, mix_rows(): pl.pallas_call(mix_kernel, out_shape=jax.ShapeDtypeStruct((mixes.shape[0]...  3.98 us
    ppermute x5, starting transfers between devices, swap(): return lax.ppermute(array, 'token', [(0, 1), (1, 0)])  3.45 us
    pallas_call x1, Pallas kernels, place_rows(): pl.pallas_call(functools.partial(route_kernel, experts, part, wide), out_...  3.41 us
  transfers between devices with their start and end apart: 7, of which 2 were waited for; matrix products, arithmetic and copies ran while one was open for 4% of the time, Pallas kernels for 0%

profile of v3, /device:TPU:1, one launch (start us, length us, event | category | flops | bytes accessed | tf_op | source)
XLA Modules:
  0.0 139.1 jit_solution(2356890543743351258)
XLA Ops:
  0.6 3.4 %shard_map.77 = bf16[1024,1792]{1,0:T(8,128)(2,1)} custom-call(s32[8,64]{1,0:T(8,128)} %bitcast.18, bf16[64,1792]{1,0:T(8,128)(2,1)} %tokens_ref.1), custom_call_target="tpu_custom_call" | custom-call | tf_op jit(solution)/shard_map/pallas_call | solution.py:59
  4.0 1.5 %collective-permute-start = (bf16[1,3584,512]{2,1,0:T(8,128)(2,1)}, bf16[1,3584,512]{2,1,0:T(8,128)(2,1)}, u32[]{:S(2)}, u32[]{:S(2)}) collective-permute-start(bf16[1,3584,512]{2,1,0:T(8,128)(2,1)} %gate_own.1), channel_id=1, source_target_pairs={{0,1},{1,0},{2,3},{3,2},{4,5},{5,4},{6,7},{7,6},{8,9},{9,8},{10,11... | collective-permute-start | bytes 11010056 | tf_op jit(solution)/shard_map/ppermute | solution.py:240
  5.5 0.1 collective-permute-start.1
  5.6 0.4 collective-permute-start.2
  6.1 10.6 %all-to-all-start = ((bf16[128,8,1792]{2,1,0:T(8,128)(2,1)}), bf16[128,8,1792]{2,1,0:T(8,128)(2,1)}, u32[]{:S(2)}, u32[]{:S(2)}) async-start(bf16[128,8,1792]{2,1,0:T(8,128)(2,1)} %bitcast.14), calls=%async_computation | async-start | bytes 7340032 | tf_op jit(solution)/shard_map/all_to_all | solution.py:267
  16.7 47.1 %all-to-all-done = bf16[128,8,1792]{2,1,0:T(8,128)(2,1)} async-done(((bf16[128,8,1792]{2,1,0:T(8,128)(2,1)}), bf16[128,8,1792]{2,1,0:T(8,128)(2,1)}, u32[]{:S(2)}, u32[]{:S(2)}) %all-to-all-start) | async-done | bytes 3670048 | tf_op jit(solution)/shard_map/all_to_all | solution.py:267
  63.8 18.2 %shard_map.78 = (bf16[64,2,8,1792]{3,2,1,0:T(8,128)(2,1)}, bf16[512,1024]{1,0:T(8,128)(2,1)}, f32[8,128]{1,0:T(8,128)}) custom-call(s32[1]{0:T(128)} %bitcast.2.core_ref, bf16[64,2,8,1792]{3,2,1,0:T(8,128)(2,1)} %bitcast.5.x_hbm, bf16[1,3584,512]{2,1,0:T(8,128)(2,1)} %gate_own.1, bf16[1,3584,512]{2,1,0:T(8,128)(2,1)} %up_own.1, ...), custom_call_target="tpu_custom_call" | custom-call | flops 11274289152 | bytes 29360128 | tf_op jit(solution)/shard_map/pallas_call | solution.py:178
  82.0 0.0 copy-start
  82.0 0.0 copy-start.1
  82.0 0.0 copy-start.2
  82.0 5.7 %all-to-all-start.1 = ((bf16[128,8,1792]{2,1,0:T(8,128)(2,1)}), bf16[128,8,1792]{2,1,0:T(8,128)(2,1)}, u32[]{:S(2)}, u32[]{:S(2)}) async-start(bf16[128,8,1792]{2,1,0:T(8,128)(2,1)} %bitcast.15), calls=%async_computation.1 | async-start | bytes 7340032 | tf_op jit(solution)/shard_map/all_to_all | solution.py:276
  87.7 0.0 copy-start.3
  87.7 1.4 collective-permute-start.4
  89.1 0.1 copy.15
  89.2 0.1 copy.18
  89.3 0.2 select_reduce_fusion
  89.5 0.1 copy.19
  89.6 0.2 copy.20
  89.8 0.2 fusion.8
  90.0 0.1 fusion
  90.1 0.1 copy.16
  90.2 0.2 copy.17
  90.4 0.1 eq.39
  90.5 0.1 reduce-precision_convert_fusion
  90.6 0.1 collective-permute-start.3
  90.7 0.7 pad_maximum_fusion.mixes_ref
  91.4 0.5 slice.6
  91.9 0.5 slice.7
  93.8 0.8 fusion.1
  94.5 2.1 %multiply_bitcast_fusion = f32[1,512,1024]{2,1,0:T(8,128)} fusion(f32[512,1024]{1,0:T(8,128)S(1)} %fusion.1, f32[]{:T(128)} %bitcast.8, bf16[512,1024]{1,0:T(8,128)(2,1)S(1)} %copy-done, s32[]{:T(128)S(6)} %select_n.20), kind=kOutput, calls=%fused_computation | convolution fusion | flops 537919488 | bytes 5767176 | tf_op jit(solution)/shard_map/dot_general | solution.py:284
  96.6 38.4 %all-to-all-done.1 = bf16[128,8,1792]{2,1,0:T(8,128)(2,1)} async-done(((bf16[128,8,1792]{2,1,0:T(8,128)(2,1)}), bf16[128,8,1792]{2,1,0:T(8,128)(2,1)}, u32[]{:S(2)}, u32[]{:S(2)}) %all-to-all-start.1) | async-done | bytes 3670048 | tf_op jit(solution)/shard_map/all_to_all | solution.py:276
  135.0 4.0 %shard_map.79 = bf16[64,1792]{1,0:T(8,128)(2,1)} custom-call(bf16[128,1024]{1,0:T(8,128)(2,1)} %pad_maximum_fusion.mixes_ref, bf16[1024,1792]{1,0:T(8,128)(2,1)} %bitcast.7.returned_hbm), custom_call_target="tpu_custom_call" | custom-call | tf_op jit(solution)/shard_map/pallas_call | solution.py:226
  (12 shorter events, 0.1 us)
Async XLA Ops:
  4.0 59.8 %collective-permute-start = (bf16[1,3584,512]{2,1,0:T(8,128)(2,1)}, bf16[1,3584,512]{2,1,0:T(8,128)(2,1)}, u32[]{:S(2)}, u32[]{:S(2)}) collective-permute-start(bf16[1,3584,512]{2,1,0:T(8,128)(2,1)} %gate_own.1), channel_id=1, source_target_pairs={{0,1},{1,0},{2,3},{3,2},{4,5},{5,4},{6,7},{7,6},{8,9},{9,8},{10,11... | collective-permute-start | bytes 11010056 | tf_op jit(solution)/shard_map/ppermute | solution.py:240
  5.5 58.3 %collective-permute-start.1 = (bf16[1,3584,512]{2,1,0:T(8,128)(2,1)}, bf16[1,3584,512]{2,1,0:T(8,128)(2,1)}, u32[]{:S(2)}, u32[]{:S(2)}) collective-permute-start(bf16[1,3584,512]{2,1,0:T(8,128)(2,1)} %up_own.1), channel_id=1, source_target_pairs={{0,1},{1,0},{2,3},{3,2},{4,5},{5,4},{6,7},{7,6},{8,9},{9,8},{10,11... | collective-permute-start | bytes 11010056 | tf_op jit(solution)/shard_map/ppermute | solution.py:240
  5.6 58.2 %collective-permute-start.2 = (bf16[1,1024,1792]{2,1,0:T(8,128)(2,1)}, bf16[1,1024,1792]{2,1,0:T(8,128)(2,1)}, u32[]{:S(2)}, u32[]{:S(2)}) collective-permute-start(bf16[1,1024,1792]{2,1,0:T(8,128)(2,1)} %down_own.1), channel_id=1, source_target_pairs={{0,1},{1,0},{2,3},{3,2},{4,5},{5,4},{6,7},{7,6},{8,9},{9,8},{10,11... | collective-permute-start | bytes 11010056 | tf_op jit(solution)/shard_map/ppermute | solution.py:240
  6.1 57.8 %all-to-all-start = ((bf16[128,8,1792]{2,1,0:T(8,128)(2,1)}), bf16[128,8,1792]{2,1,0:T(8,128)(2,1)}, u32[]{:S(2)}, u32[]{:S(2)}) async-start(bf16[128,8,1792]{2,1,0:T(8,128)(2,1)} %bitcast.14), calls=%async_computation | async-start | bytes 7340032 | tf_op jit(solution)/shard_map/all_to_all | solution.py:267
  82.0 5.7 %copy-start = (bf16[512,1024]{1,0:T(8,128)(2,1)S(1)}, bf16[512,1024]{1,0:T(8,128)(2,1)}, u32[]{:S(2)}) copy-start(bf16[512,1024]{1,0:T(8,128)(2,1)} %get-tuple-element.13) | copy-start | bytes 3145732
  82.0 7.1 %copy-start.1 = (s32[64,8]{0,1:T(8,128)S(1)}, s32[64,8]{0,1:T(8,128)}, u32[]{:S(2)}) copy-start(s32[64,8]{0,1:T(8,128)} %param.7) | copy-start | bytes 6148
  82.0 7.2 %copy-start.2 = (f32[64,8]{0,1:T(8,128)S(1)}, f32[64,8]{0,1:T(8,128)}, u32[]{:S(2)}) copy-start(f32[64,8]{0,1:T(8,128)} %param.8) | copy-start | bytes 6148
  82.0 53.0 %all-to-all-start.1 = ((bf16[128,8,1792]{2,1,0:T(8,128)(2,1)}), bf16[128,8,1792]{2,1,0:T(8,128)(2,1)}, u32[]{:S(2)}, u32[]{:S(2)}) async-start(bf16[128,8,1792]{2,1,0:T(8,128)(2,1)} %bitcast.15), calls=%async_computation.1 | async-start | bytes 7340032 | tf_op jit(solution)/shard_map/all_to_all | solution.py:276
  87.7 2.9 %copy-start.3 = (f32[8,128]{1,0:T(8,128)S(1)}, f32[8,128]{1,0:T(8,128)}, u32[]{:S(2)}) copy-start(f32[8,128]{1,0:T(8,128)} %get-tuple-element.12) | copy-start | bytes 12292
  87.7 6.0 %collective-permute-start.4 = (bf16[512,1024]{1,0:T(8,128)(2,1)S(1)}, bf16[512,1024]{1,0:T(8,128)(2,1)S(1)}, u32[]{:S(2)}, u32[]{:S(2)}) collective-permute-start(bf16[512,1024]{1,0:T(8,128)(2,1)S(1)} %copy-done), channel_id=1, source_target_pairs={{0,1},{1,0},{2,3},{3,2},{4,5},{5,4},{6,7},{7,6},{8,9},{9,8},{10,11... | collective-permute-start | bytes 3145736 | tf_op jit(solution)/shard_map/ppermute | solution.py:240
  90.6 1.3 collective-permute-start.3

commit v4 on v3

--- a/solution.py
+++ b/solution.py
@@ -126,27 +126,39 @@
 
     ahead(LOOKAHEAD)
 
+    def features(f):
+        return x[f].reshape(rows, half)
+
     def product(i):
-        if i == 0:
-            ready(2)
-            total = jnp.dot(x[0, :, :, :cut].reshape(rows, cut), first[0, 0, :cut], preferred_element_type=jnp.float32)
-            ready(4)
-            total = total + jnp.dot(x[0, :, :, cut:].reshape(rows, half - cut), first[0, 0, cut:], preferred_element_type=jnp.float32)
-        else:
-            ready(5 + 2 * i)
-            total = jnp.dot(x[0].reshape(rows, half), first[i, 0], preferred_element_type=jnp.float32)
-        ready(6 + 2 * i)
-        return total + jnp.dot(x[1].reshape(rows, half), first[i, 1], preferred_element_type=jnp.float32)
-
-    for side in range(2):
-        gate = product(2 * side)
-        if side == 0:
-            valid = x[0, :, :, :128].astype(jnp.float32).reshape(rows, 128)[:, :1] < EMPTY / 2
-            count_ref[...] = jnp.full(count_ref.shape, jnp.sum(valid.astype(jnp.float32)))
-        upper = product(2 * side + 1)
+        return jnp.dot(
+            features(0), first[i, 0], preferred_element_type=jnp.float32
+        ) + jnp.dot(features(1), first[i, 1], preferred_element_type=jnp.float32)
+
+    def keep(side, gate, upper):
         hidden = jnp.where(valid, gate / (1.0 + jnp.exp(-gate)) * upper, 0.0)
         base = (core if side == 0 else 1 - core) * ff_half
         hid_ref[:, pl.ds(pl.multiple_of(base, ff_half), ff_half)] = hidden.astype(hid_ref.dtype)
+
+    ready(2)
+    gate = jnp.dot(
+        x[0, :, :, :cut].reshape(rows, cut), first[0, 0, :cut], preferred_element_type=jnp.float32
+    )
+    ready(4)
+    gate = gate + jnp.dot(
+        x[0, :, :, cut:].reshape(rows, half - cut), first[0, 0, cut:],
+        preferred_element_type=jnp.float32,
+    )
+    ready(6)
+    gate = gate + jnp.dot(features(1), first[0, 1], preferred_element_type=jnp.float32)
+    valid = x[0, :, :, :128].astype(jnp.float32).reshape(rows, 128)[:, :1] < EMPTY / 2
+    count_ref[...] = jnp.full(count_ref.shape, jnp.sum(valid.astype(jnp.float32)))
+    ready(8)
+    upper = product(1)
+    ready(10)
+    keep(0, gate, upper)
+    gate = product(2)
+    ready(12)
+    keep(1, gate, product(3))
     copies = []
     for side in range(2):
         ready(13 + side)
@@ -202,40 +214,6 @@
     )(core, x, gate_own, up_own, gate_other, up_other, down_own, down_other)
 
 
-def mix_kernel(mixes_ref, returned_hbm, out_ref, returned, sems):
-    tok_rows = out_ref.shape[0]
-    parts, rows, _ = returned.shape
-    copies = []
-    for n in range(parts):
-        span = pl.ds(n * rows, rows)
-        copies.append(pltpu.make_async_copy(returned_hbm.at[span], returned.at[n], sems.at[n]))
-        copies[-1].start()
-    total = None
-    for n, copy in enumerate(copies):
-        copy.wait()
-        both = jnp.dot(
-            mixes_ref[:, n * rows : (n + 1) * rows], returned[n], preferred_element_type=jnp.float32
-        )
-        total = both if total is None else total + both
-    out_ref[...] = (total[:tok_rows] + total[tok_rows:]).astype(out_ref.dtype)
-
-
-def mix_rows(mixes, returned):
-    rows, half = returned.shape
-    parts = 4
-    return pl.pallas_call(
-        mix_kernel,
-        out_shape=jax.ShapeDtypeStruct((mixes.shape[0] // 2, half), jnp.bfloat16),
-        in_specs=[pl.BlockSpec(memory_space=pltpu.VMEM), pl.BlockSpec(memory_space=pltpu.HBM)],
-        out_specs=pl.BlockSpec(memory_space=pltpu.VMEM),
-        scratch_shapes=[
-            pltpu.VMEM((parts, rows // parts, half), jnp.bfloat16),
-            pltpu.SemaphoreType.DMA((parts,)),
-        ],
-        compiler_params=pltpu.CompilerParams(vmem_limit_bytes=VMEM_LIMIT),
-    )(mixes, returned)
-
-
 def swap(array):
     return lax.ppermute(array, "token", [(0, 1), (1, 0)])
 
@@ -254,7 +232,7 @@
     place = key[:, :, None] == slot
     mixes = jnp.where(place, weight[:, :, None], 0.0).reshape(tok_rows, -1)
     high = lax.reduce_precision(mixes, 8, 7)
-    return jnp.concatenate([high, mixes - high], axis=0).astype(jnp.bfloat16)
+    return high.astype(jnp.bfloat16), (mixes - high).astype(jnp.bfloat16)
 
 
 def shards(tokens, routes, mixing, gate_weight, up_weight, down_weight):
@@ -287,7 +265,9 @@
 
     total = count[0, 0] + count_other[0, 0]
     hessian = (2.0 / total * (outer(hidden) + outer(hidden_other)))[None]
-    mixed = mix_rows(mix_table(routes, mixing, experts, part), returned)
+    high, low = mix_table(routes, mixing, experts, part)
+    mixed = jnp.dot(jnp.concatenate([high, low]), returned, preferred_element_type=jnp.float32)
+    mixed = (mixed[:tok_rows] + mixed[tok_rows:]).astype(jnp.bfloat16)
     return mixed, hessian
 
 

time: 139 us -> 138 us (level)
  Pallas kernels: 25.5 us -> 20.9 us
  matrix products: 2.97 us -> 5.77 us
    pallas_call x1 -> x0, Pallas kernels: 3.98 us -> none  [mix_rows(): pl.pallas_call(mix_kernel, out_shape=jax.ShapeDtypeStruct((mixes.shape[0]...]
    dot_general x0 -> x1, matrix products: none -> 2.8 us  [shards(): jnp.dot(jnp.concatenate([high, low]), returned, preferred_element_type=jn...]
  transfers between devices with their start and end apart: 7 -> 7, of which waited for: 2 -> 3; matrix products, arithmetic and copies ran while one was open for 4% -> 4% of each run, Pallas kernels for 0% -> 0%
where the time goes in v4:
time: 138 us
  waiting for transfers between devices  86.6 us (63%)
  Pallas kernels  20.9 us (15%)
  starting transfers between devices  19.5 us (14%)
  matrix products  5.77 us (4%)
  between operations  2.1 us (2%)
  local copies, waits for them, and re-layouts  1.46 us (1%)
    all_to_all x1, waiting for transfers between devices, shards(): received = lax.all_to_all(outgoing, ('expert', 'token'), 0, 0, tiled=True)  47.1 us
    all_to_all x1, waiting for transfers between devices, shards(): lax.all_to_all(out.reshape(2 * experts, part, half), ('expert', 'token'),...  38.9 us
    pallas_call x1, Pallas kernels, run_experts(): pl.pallas_call(expert_kernel, out_shape=(jax.ShapeDtypeStruct((groups, 2,...  17.5 us
    all_to_all x1, starting transfers between devices, shards(): received = lax.all_to_all(outgoing, ('expert', 'token'), 0, 0, tiled=True)  10.6 us
    all_to_all x1, starting transfers between devices, shards(): lax.all_to_all(out.reshape(2 * experts, part, half), ('expert', 'token'),...  5.5 us
    ppermute x5, starting transfers between devices, swap(): return lax.ppermute(array, 'token', [(0, 1), (1, 0)])  3.44 us
    pallas_call x1, Pallas kernels, place_rows(): pl.pallas_call(functools.partial(route_kernel, experts, part, wide), out_...  3.43 us
    dot_general x2, matrix products, outer(): lax.dot_general(own, array, (((0,), (0,)), ((), ())), preferred_element_t...  2.84 us
  transfers between devices with their start and end apart: 7, of which 3 were waited for; matrix products, arithmetic and copies ran while one was open for 4% of the time, Pallas kernels for 0%

profile of v4, /device:TPU:1, one launch (start us, length us, event | category | flops | bytes accessed | tf_op | source)
XLA Modules:
  0.0 137.7 jit_solution(15073132591487238840)
XLA Ops:
  0.6 3.4 %shard_map.77 = bf16[1024,1792]{1,0:T(8,128)(2,1)} custom-call(s32[8,64]{1,0:T(8,128)} %bitcast.28, bf16[64,1792]{1,0:T(8,128)(2,1)} %tokens_ref.1), custom_call_target="tpu_custom_call" | custom-call | tf_op jit(solution)/shard_map/pallas_call | solution.py:59
  4.1 1.5 %collective-permute-start = (bf16[1,3584,512]{2,1,0:T(8,128)(2,1)}, bf16[1,3584,512]{2,1,0:T(8,128)(2,1)}, u32[]{:S(2)}, u32[]{:S(2)}) collective-permute-start(bf16[1,3584,512]{2,1,0:T(8,128)(2,1)} %gate_own.1), channel_id=1, source_target_pairs={{0,1},{1,0},{2,3},{3,2},{4,5},{5,4},{6,7},{7,6},{8,9},{9,8},{10,11... | collective-permute-start | bytes 11010056 | tf_op jit(solution)/shard_map/ppermute | solution.py:218
  5.6 0.1 collective-permute-start.1
  5.7 0.4 collective-permute-start.2
  6.1 10.6 %all-to-all-start = ((bf16[128,8,1792]{2,1,0:T(8,128)(2,1)}), bf16[128,8,1792]{2,1,0:T(8,128)(2,1)}, u32[]{:S(2)}, u32[]{:S(2)}) async-start(bf16[128,8,1792]{2,1,0:T(8,128)(2,1)} %bitcast.26), calls=%async_computation | async-start | bytes 7340032 | tf_op jit(solution)/shard_map/all_to_all | solution.py:245
  16.7 47.1 %all-to-all-done = bf16[128,8,1792]{2,1,0:T(8,128)(2,1)} async-done(((bf16[128,8,1792]{2,1,0:T(8,128)(2,1)}), bf16[128,8,1792]{2,1,0:T(8,128)(2,1)}, u32[]{:S(2)}, u32[]{:S(2)}) %all-to-all-start) | async-done | bytes 3670048 | tf_op jit(solution)/shard_map/all_to_all | solution.py:245
  63.8 0.0 collective-permute-done.gate_other
  63.8 17.5 %shard_map.78 = (bf16[64,2,8,1792]{3,2,1,0:T(8,128)(2,1)}, bf16[512,1024]{1,0:T(8,128)(2,1)}, f32[8,128]{1,0:T(8,128)}) custom-call(s32[1]{0:T(128)} %bitcast.2.core_ref, bf16[64,2,8,1792]{3,2,1,0:T(8,128)(2,1)} %bitcast.5.x_hbm, bf16[1,3584,512]{2,1,0:T(8,128)(2,1)} %gate_own.1, bf16[1,3584,512]{2,1,0:T(8,128)(2,1)} %up_own.1, ...), custom_call_target="tpu_custom_call" | custom-call | flops 11274289152 | bytes 29360128 | tf_op jit(solution)/shard_map/pallas_call | solution.py:190
  81.3 0.0 copy-start
  81.3 0.0 copy-start.1
  81.3 0.0 copy-start.2
  81.3 0.0 copy-start.3
  81.4 5.5 %all-to-all-start.1 = ((bf16[128,8,1792]{2,1,0:T(8,128)(2,1)}), bf16[128,8,1792]{2,1,0:T(8,128)(2,1)}, u32[]{:S(2)}, u32[]{:S(2)}) async-start(bf16[128,8,1792]{2,1,0:T(8,128)(2,1)} %bitcast.27), calls=%async_computation.1 | async-start | bytes 7340032 | tf_op jit(solution)/shard_map/all_to_all | solution.py:254
  86.9 1.4 collective-permute-start.4
  88.2 0.1 copy.13
  88.3 0.1 copy.15
  88.4 0.2 fusion.14
  88.6 0.1 fusion.2
  88.7 0.1 collective-permute-start.3
  88.8 0.2 select_reduce_fusion
  89.0 0.1 copy.16
  89.1 0.1 copy.14
  89.2 0.1 eq.39
  89.3 0.2 reduce-precision_convert_fusion
  89.5 0.5 slice.14
  90.0 0.5 collective-permute-done.3
  90.5 0.5 slice.15
  92.4 0.8 fusion.4
  93.1 2.1 %multiply_bitcast_fusion = f32[1,512,1024]{2,1,0:T(8,128)} fusion(f32[512,1024]{1,0:T(8,128)S(1)} %fusion.4, f32[]{:T(128)} %bitcast.8, bf16[512,1024]{1,0:T(8,128)(2,1)S(1)} %copy-done, s32[]{:T(128)S(6)} %select_n.20), kind=kOutput, calls=%fused_computation.2 | convolution fusion | flops 537919488 | bytes 5767176 | tf_op jit(solution)/shard_map/dot_general | solution.py:262
  95.2 38.9 %all-to-all-done.1 = bf16[128,8,1792]{2,1,0:T(8,128)(2,1)} async-done(((bf16[128,8,1792]{2,1,0:T(8,128)(2,1)}), bf16[128,8,1792]{2,1,0:T(8,128)(2,1)}, u32[]{:S(2)}, u32[]{:S(2)}) %all-to-all-start.1) | async-done | bytes 3670048 | tf_op jit(solution)/shard_map/all_to_all | solution.py:254
  134.1 2.8 %fusion = f32[128,1792]{1,0:T(8,128)S(1)} fusion(bf16[128,8,1792]{2,1,0:T(8,128)(2,1)} %all-to-all-done.1, bf16[64,1024]{0,1:T(8,128)(2,1)S(1)} %get-tuple-element.15, bf16[64,1024]{0,1:T(8,128)(2,1)S(1)} %get-tuple-element.14), kind=kOutput, calls=%fused_computation | convolution fusion | flops 470286336 | bytes 4849664 | tf_op jit(solution)/shard_map/dot_general | solution.py:269
  136.9 0.7 fusion.10
  (8 shorter events, 0.0 us)
Async XLA Ops:
  4.1 59.8 %collective-permute-start = (bf16[1,3584,512]{2,1,0:T(8,128)(2,1)}, bf16[1,3584,512]{2,1,0:T(8,128)(2,1)}, u32[]{:S(2)}, u32[]{:S(2)}) collective-permute-start(bf16[1,3584,512]{2,1,0:T(8,128)(2,1)} %gate_own.1), channel_id=1, source_target_pairs={{0,1},{1,0},{2,3},{3,2},{4,5},{5,4},{6,7},{7,6},{8,9},{9,8},{10,11... | collective-permute-start | bytes 11010056 | tf_op jit(solution)/shard_map/ppermute | solution.py:218
  5.6 58.3 %collective-permute-start.1 = (bf16[1,3584,512]{2,1,0:T(8,128)(2,1)}, bf16[1,3584,512]{2,1,0:T(8,128)(2,1)}, u32[]{:S(2)}, u32[]{:S(2)}) collective-permute-start(bf16[1,3584,512]{2,1,0:T(8,128)(2,1)} %up_own.1), channel_id=1, source_target_pairs={{0,1},{1,0},{2,3},{3,2},{4,5},{5,4},{6,7},{7,6},{8,9},{9,8},{10,11... | collective-permute-start | bytes 11010056 | tf_op jit(solution)/shard_map/ppermute | solution.py:218
  5.7 58.2 %collective-permute-start.2 = (bf16[1,1024,1792]{2,1,0:T(8,128)(2,1)}, bf16[1,1024,1792]{2,1,0:T(8,128)(2,1)}, u32[]{:S(2)}, u32[]{:S(2)}) collective-permute-start(bf16[1,1024,1792]{2,1,0:T(8,128)(2,1)} %down_own.1), channel_id=1, source_target_pairs={{0,1},{1,0},{2,3},{3,2},{4,5},{5,4},{6,7},{7,6},{8,9},{9,8},{10,11... | collective-permute-start | bytes 11010056 | tf_op jit(solution)/shard_map/ppermute | solution.py:218
  6.1 57.7 %all-to-all-start = ((bf16[128,8,1792]{2,1,0:T(8,128)(2,1)}), bf16[128,8,1792]{2,1,0:T(8,128)(2,1)}, u32[]{:S(2)}, u32[]{:S(2)}) async-start(bf16[128,8,1792]{2,1,0:T(8,128)(2,1)} %bitcast.26), calls=%async_computation | async-start | bytes 7340032 | tf_op jit(solution)/shard_map/all_to_all | solution.py:245
  81.3 5.6 %copy-start = (bf16[512,1024]{1,0:T(8,128)(2,1)S(1)}, bf16[512,1024]{1,0:T(8,128)(2,1)}, u32[]{:S(2)}) copy-start(bf16[512,1024]{1,0:T(8,128)(2,1)} %get-tuple-element.13) | copy-start | bytes 3145732
  81.3 6.9 %copy-start.1 = (s32[64,8]{0,1:T(8,128)S(1)}, s32[64,8]{0,1:T(8,128)}, u32[]{:S(2)}) copy-start(s32[64,8]{0,1:T(8,128)} %param.7) | copy-start | bytes 6148
  81.3 7.0 %copy-start.2 = (f32[64,8]{0,1:T(8,128)S(1)}, f32[64,8]{0,1:T(8,128)}, u32[]{:S(2)}) copy-start(f32[64,8]{0,1:T(8,128)} %param.8) | copy-start | bytes 6148
  81.3 7.4 %copy-start.3 = (f32[8,128]{1,0:T(8,128)S(1)}, f32[8,128]{1,0:T(8,128)}, u32[]{:S(2)}) copy-start(f32[8,128]{1,0:T(8,128)} %get-tuple-element.12) | copy-start | bytes 12292
  81.4 52.8 %all-to-all-start.1 = ((bf16[128,8,1792]{2,1,0:T(8,128)(2,1)}), bf16[128,8,1792]{2,1,0:T(8,128)(2,1)}, u32[]{:S(2)}, u32[]{:S(2)}) async-start(bf16[128,8,1792]{2,1,0:T(8,128)(2,1)} %bitcast.27), calls=%async_computation.1 | async-start | bytes 7340032 | tf_op jit(solution)/shard_map/all_to_all | solution.py:254
  86.9 5.5 %collective-permute-start.4 = (bf16[512,1024]{1,0:T(8,128)(2,1)S(1)}, bf16[512,1024]{1,0:T(8,128)(2,1)S(1)}, u32[]{:S(2)}, u32[]{:S(2)}) collective-permute-start(bf16[512,1024]{1,0:T(8,128)(2,1)S(1)} %copy-done), channel_id=1, source_target_pairs={{0,1},{1,0},{2,3},{3,2},{4,5},{5,4},{6,7},{7,6},{8,9},{9,8},{10,11... | collective-permute-start | bytes 3145736 | tf_op jit(solution)/shard_map/ppermute | solution.py:218
  88.7 1.8 %collective-permute-start.3 = (f32[8,128]{1,0:T(8,128)S(1)}, f32[8,128]{1,0:T(8,128)S(1)}, u32[]{:S(2)}, u32[]{:S(2)}) collective-permute-start(f32[8,128]{1,0:T(8,128)S(1)} %copy-done.3), channel_id=1, source_target_pairs={{0,1},{1,0},{2,3},{3,2},{4,5},{5,4},{6,7},{7,6},{8,9},{9,8},{10,11... | collective-permute-start | bytes 12296 | tf_op jit(solution)/shard_map/ppermute | solution.py:218

commit v5 on v4

--- a/solution.py
+++ b/solution.py
@@ -12,9 +12,14 @@
 VMEM_LIMIT = 61 * 1024 * 1024
 
 
-def route_kernel(experts, part, wide, routes_ref, tokens_ref, out_hbm, out, sems):
+def route_kernel(experts, part, wide, routes_hbm, tokens_hbm, out_hbm, routes_ref, tokens_ref, out, sems):
     tok_rows, half = tokens_ref.shape
     steps = half // wide
+    load_routes = pltpu.make_async_copy(routes_hbm, routes_ref, sems.at[2 * steps])
+    load_tokens = pltpu.make_async_copy(tokens_hbm, tokens_ref, sems.at[2 * steps + 1])
+    load_routes.start()
+    load_tokens.start()
+    load_routes.wait()
     names = lax.broadcasted_iota(jnp.int32, (experts, tok_rows), 0)
     chosen = names == routes_ref[0:1, :]
     for k in range(1, routes_ref.shape[0]):
@@ -31,6 +36,7 @@
     rows = group * 2 * part
     lane = lax.broadcasted_iota(jnp.int32, (rows, wide), 1)
     slot = lax.broadcasted_iota(jnp.int32, (group, 2 * part, tok_rows), 1).astype(jnp.float32)
+    load_tokens.wait()
     copies = []
     for c in range(2):
         place = jnp.where(key[c * group : (c + 1) * group, None, :] == slot, 1.0, 0.0)
@@ -59,10 +65,13 @@
     return pl.pallas_call(
         functools.partial(route_kernel, experts, part, wide),
         out_shape=jax.ShapeDtypeStruct(shape, jnp.bfloat16),
-        in_specs=[pl.BlockSpec(memory_space=pltpu.VMEM)] * 2,
+        in_specs=[pl.BlockSpec(memory_space=pltpu.HBM)] * 2,
         out_specs=pl.BlockSpec(memory_space=pltpu.HBM),
         scratch_shapes=[
-            pltpu.VMEM(shape, jnp.bfloat16), pltpu.SemaphoreType.DMA((2 * (half // wide),))
+            pltpu.VMEM(routes.shape, routes.dtype),
+            pltpu.VMEM(tokens.shape, tokens.dtype),
+            pltpu.VMEM(shape, jnp.bfloat16),
+            pltpu.SemaphoreType.DMA((2 * (half // wide) + 2,)),
         ],
         compiler_params=pltpu.CompilerParams(vmem_limit_bytes=VMEM_LIMIT),
     )(routes, tokens)
@@ -70,7 +79,8 @@
 
 def expert_kernel(
     core_ref, x_hbm, gate_own, up_own, gate_other, up_other, down_own, down_other,
-    out_hbm, hid_ref, count_ref, x, first, second, outs, x_sems, f_sems, s_sems, o_sems,
+    out_hbm, hid_hbm, count_hbm, x, first, second, outs, hid_ref, count_ref,
+    x_sems, f_sems, s_sems, o_sems, e_sems,
 ):
     core = core_ref[0]
     _, groups, part, half = x.shape
@@ -152,6 +162,8 @@
     gate = gate + jnp.dot(features(1), first[0, 1], preferred_element_type=jnp.float32)
     valid = x[0, :, :, :128].astype(jnp.float32).reshape(rows, 128)[:, :1] < EMPTY / 2
     count_ref[...] = jnp.full(count_ref.shape, jnp.sum(valid.astype(jnp.float32)))
+    copies = [pltpu.make_async_copy(count_ref, count_hbm, e_sems.at[0])]
+    copies[0].start()
     ready(8)
     upper = product(1)
     ready(10)
@@ -159,7 +171,8 @@
     gate = product(2)
     ready(12)
     keep(1, gate, product(3))
-    copies = []
+    copies.append(pltpu.make_async_copy(hid_ref, hid_hbm, e_sems.at[1]))
+    copies[1].start()
     for side in range(2):
         ready(13 + side)
         target = core if side == 0 else 1 - core
@@ -185,7 +198,6 @@
     width = 2 * half
     ff_half = gate_own.shape[2]
     ff = 2 * ff_half
-    whole = pl.BlockSpec(memory_space=pltpu.VMEM)
     far = pl.BlockSpec(memory_space=pltpu.HBM)
     return pl.pallas_call(
         expert_kernel,
@@ -195,16 +207,19 @@
             jax.ShapeDtypeStruct((8, 128), jnp.float32),
         ),
         in_specs=[pl.BlockSpec(memory_space=pltpu.SMEM)] + [far] * 7,
-        out_specs=(far, whole, whole),
+        out_specs=(far, far, far),
         scratch_shapes=[
             pltpu.VMEM((2, groups, part, half), jnp.bfloat16),
             pltpu.VMEM((4, 2, half, ff_half), jnp.bfloat16),
             pltpu.VMEM((2, ff, half), jnp.bfloat16),
             pltpu.VMEM((2, groups, part, half), jnp.bfloat16),
+            pltpu.VMEM((rows, ff), jnp.bfloat16),
+            pltpu.VMEM((8, 128), jnp.float32),
             pltpu.SemaphoreType.DMA((3,)),
             pltpu.SemaphoreType.DMA((9,)),
             pltpu.SemaphoreType.DMA((2,)),
             pltpu.SemaphoreType.DMA((2 * (half // 256),)),
+            pltpu.SemaphoreType.DMA((2,)),
         ],
         compiler_params=pltpu.CompilerParams(vmem_limit_bytes=VMEM_LIMIT),
         cost_estimate=pl.CostEstimate(

time: 138 us -> 137 us (level)
  no operation moved by 1% of the time
where the time goes in v5:
time: 137 us
  waiting for transfers between devices  86.6 us (63%)
  Pallas kernels  19.8 us (14%)
  starting transfers between devices  19.5 us (14%)
  matrix products  5.78 us (4%)
  between operations  2.1 us (2%)
  local copies, waits for them, and re-layouts  1.46 us (1%)
    all_to_all x1, waiting for transfers between devices, shards(): received = lax.all_to_all(outgoing, ('expert', 'token'), 0, 0, tiled=True)  47.1 us
    all_to_all x1, waiting for transfers between devices, shards(): lax.all_to_all(out.reshape(2 * experts, part, half), ('expert', 'token'),...  38.9 us
    pallas_call x1, Pallas kernels, run_experts(): pl.pallas_call(expert_kernel, out_shape=(jax.ShapeDtypeStruct((groups, 2,...  16.5 us
    all_to_all x1, starting transfers between devices, shards(): received = lax.all_to_all(outgoing, ('expert', 'token'), 0, 0, tiled=True)  10.6 us
    all_to_all x1, starting transfers between devices, shards(): lax.all_to_all(out.reshape(2 * experts, part, half), ('expert', 'token'),...  5.49 us
    ppermute x5, starting transfers between devices, swap(): return lax.ppermute(array, 'token', [(0, 1), (1, 0)])  3.44 us
    pallas_call x1, Pallas kernels, place_rows(): pl.pallas_call(functools.partial(route_kernel, experts, part, wide), out_...  3.32 us
    dot_general x2, matrix products, outer(): lax.dot_general(own, array, (((0,), (0,)), ((), ())), preferred_element_t...  2.84 us
  transfers between devices with their start and end apart: 7, of which 3 were waited for; matrix products, arithmetic and copies ran while one was open for 4% of the time, Pallas kernels for 0%

profile of v5, /device:TPU:1, one launch (start us, length us, event | category | flops | bytes accessed | tf_op | source)
XLA Modules:
  0.0 136.6 jit_solution(2056911304858574089)
XLA Ops:
  0.6 3.3 %shard_map.77 = bf16[1024,1792]{1,0:T(8,128)(2,1)} custom-call(s32[8,64]{1,0:T(8,128)} %bitcast.28, bf16[64,1792]{1,0:T(8,128)(2,1)} %tokens_hbm.1), custom_call_target="tpu_custom_call" | custom-call | tf_op jit(solution)/shard_map/pallas_call | solution.py:65
  4.0 1.5 %collective-permute-start = (bf16[1,3584,512]{2,1,0:T(8,128)(2,1)}, bf16[1,3584,512]{2,1,0:T(8,128)(2,1)}, u32[]{:S(2)}, u32[]{:S(2)}) collective-permute-start(bf16[1,3584,512]{2,1,0:T(8,128)(2,1)} %gate_own.1), channel_id=1, source_target_pairs={{0,1},{1,0},{2,3},{3,2},{4,5},{5,4},{6,7},{7,6},{8,9},{9,8},{10,11... | collective-permute-start | bytes 11010056 | tf_op jit(solution)/shard_map/ppermute | solution.py:233
  5.5 0.1 collective-permute-start.1
  5.6 0.4 collective-permute-start.2
  6.0 10.6 %all-to-all-start = ((bf16[128,8,1792]{2,1,0:T(8,128)(2,1)}), bf16[128,8,1792]{2,1,0:T(8,128)(2,1)}, u32[]{:S(2)}, u32[]{:S(2)}) async-start(bf16[128,8,1792]{2,1,0:T(8,128)(2,1)} %bitcast.26), calls=%async_computation | async-start | bytes 7340032 | tf_op jit(solution)/shard_map/all_to_all | solution.py:260
  16.6 47.1 %all-to-all-done = bf16[128,8,1792]{2,1,0:T(8,128)(2,1)} async-done(((bf16[128,8,1792]{2,1,0:T(8,128)(2,1)}), bf16[128,8,1792]{2,1,0:T(8,128)(2,1)}, u32[]{:S(2)}, u32[]{:S(2)}) %all-to-all-start) | async-done | bytes 3670048 | tf_op jit(solution)/shard_map/all_to_all | solution.py:260
  63.7 0.0 collective-permute-done.gate_other
  63.7 16.5 %shard_map.78 = (bf16[64,2,8,1792]{3,2,1,0:T(8,128)(2,1)}, bf16[512,1024]{1,0:T(8,128)(2,1)}, f32[8,128]{1,0:T(8,128)}) custom-call(s32[1]{0:T(128)} %bitcast.2.core_ref, bf16[64,2,8,1792]{3,2,1,0:T(8,128)(2,1)} %bitcast.5.x_hbm, bf16[1,3584,512]{2,1,0:T(8,128)(2,1)} %gate_own.1, bf16[1,3584,512]{2,1,0:T(8,128)(2,1)} %up_own.1, ...), custom_call_target="tpu_custom_call" | custom-call | flops 11274289152 | bytes 29360128 | tf_op jit(solution)/shard_map/pallas_call | solution.py:202
  80.2 0.0 copy-start
  80.3 0.0 copy-start.1
  80.3 0.0 copy-start.2
  80.3 0.0 copy-start.3
  80.3 5.5 %all-to-all-start.1 = ((bf16[128,8,1792]{2,1,0:T(8,128)(2,1)}), bf16[128,8,1792]{2,1,0:T(8,128)(2,1)}, u32[]{:S(2)}, u32[]{:S(2)}) async-start(bf16[128,8,1792]{2,1,0:T(8,128)(2,1)} %bitcast.27), calls=%async_computation.1 | async-start | bytes 7340032 | tf_op jit(solution)/shard_map/all_to_all | solution.py:269
  85.8 1.4 collective-permute-start.4
  87.2 0.1 copy.13
  87.2 0.1 copy.15
  87.3 0.2 fusion.14
  87.5 0.1 fusion.2
  87.6 0.1 collective-permute-start.3
  87.7 0.2 select_reduce_fusion
  87.9 0.1 copy.16
  88.0 0.1 copy.14
  88.1 0.1 eq.39
  88.2 0.2 reduce-precision_convert_fusion
  88.4 0.5 slice.14
  88.9 0.5 collective-permute-done.3
  89.4 0.5 slice.15
  91.3 0.8 fusion.4
  92.1 2.1 %multiply_bitcast_fusion = f32[1,512,1024]{2,1,0:T(8,128)} fusion(f32[512,1024]{1,0:T(8,128)S(1)} %fusion.4, f32[]{:T(128)} %bitcast.8, bf16[512,1024]{1,0:T(8,128)(2,1)S(1)} %copy-done, s32[]{:T(128)S(6)} %select_n.20), kind=kOutput, calls=%fused_computation.2 | convolution fusion | flops 537919488 | bytes 5767176 | tf_op jit(solution)/shard_map/dot_general | solution.py:277
  94.2 38.9 %all-to-all-done.1 = bf16[128,8,1792]{2,1,0:T(8,128)(2,1)} async-done(((bf16[128,8,1792]{2,1,0:T(8,128)(2,1)}), bf16[128,8,1792]{2,1,0:T(8,128)(2,1)}, u32[]{:S(2)}, u32[]{:S(2)}) %all-to-all-start.1) | async-done | bytes 3670048 | tf_op jit(solution)/shard_map/all_to_all | solution.py:269
  133.1 2.8 %fusion = f32[128,1792]{1,0:T(8,128)S(1)} fusion(bf16[128,8,1792]{2,1,0:T(8,128)(2,1)} %all-to-all-done.1, bf16[64,1024]{0,1:T(8,128)(2,1)S(1)} %get-tuple-element.15, bf16[64,1024]{0,1:T(8,128)(2,1)S(1)} %get-tuple-element.14), kind=kOutput, calls=%fused_computation | convolution fusion | flops 470286336 | bytes 4849664 | tf_op jit(solution)/shard_map/dot_general | solution.py:284
  135.9 0.7 fusion.10
  (8 shorter events, 0.0 us)
Async XLA Ops:
  4.0 59.8 %collective-permute-start = (bf16[1,3584,512]{2,1,0:T(8,128)(2,1)}, bf16[1,3584,512]{2,1,0:T(8,128)(2,1)}, u32[]{:S(2)}, u32[]{:S(2)}) collective-permute-start(bf16[1,3584,512]{2,1,0:T(8,128)(2,1)} %gate_own.1), channel_id=1, source_target_pairs={{0,1},{1,0},{2,3},{3,2},{4,5},{5,4},{6,7},{7,6},{8,9},{9,8},{10,11... | collective-permute-start | bytes 11010056 | tf_op jit(solution)/shard_map/ppermute | solution.py:233
  5.5 58.3 %collective-permute-start.1 = (bf16[1,3584,512]{2,1,0:T(8,128)(2,1)}, bf16[1,3584,512]{2,1,0:T(8,128)(2,1)}, u32[]{:S(2)}, u32[]{:S(2)}) collective-permute-start(bf16[1,3584,512]{2,1,0:T(8,128)(2,1)} %up_own.1), channel_id=1, source_target_pairs={{0,1},{1,0},{2,3},{3,2},{4,5},{5,4},{6,7},{7,6},{8,9},{9,8},{10,11... | collective-permute-start | bytes 11010056 | tf_op jit(solution)/shard_map/ppermute | solution.py:233
  5.6 58.2 %collective-permute-start.2 = (bf16[1,1024,1792]{2,1,0:T(8,128)(2,1)}, bf16[1,1024,1792]{2,1,0:T(8,128)(2,1)}, u32[]{:S(2)}, u32[]{:S(2)}) collective-permute-start(bf16[1,1024,1792]{2,1,0:T(8,128)(2,1)} %down_own.1), channel_id=1, source_target_pairs={{0,1},{1,0},{2,3},{3,2},{4,5},{5,4},{6,7},{7,6},{8,9},{9,8},{10,11... | collective-permute-start | bytes 11010056 | tf_op jit(solution)/shard_map/ppermute | solution.py:233
  6.0 57.7 %all-to-all-start = ((bf16[128,8,1792]{2,1,0:T(8,128)(2,1)}), bf16[128,8,1792]{2,1,0:T(8,128)(2,1)}, u32[]{:S(2)}, u32[]{:S(2)}) async-start(bf16[128,8,1792]{2,1,0:T(8,128)(2,1)} %bitcast.26), calls=%async_computation | async-start | bytes 7340032 | tf_op jit(solution)/shard_map/all_to_all | solution.py:260
  80.2 5.6 %copy-start = (bf16[512,1024]{1,0:T(8,128)(2,1)S(1)}, bf16[512,1024]{1,0:T(8,128)(2,1)}, u32[]{:S(2)}) copy-start(bf16[512,1024]{1,0:T(8,128)(2,1)} %get-tuple-element.13) | copy-start | bytes 3145732
  80.3 6.9 %copy-start.1 = (s32[64,8]{0,1:T(8,128)S(1)}, s32[64,8]{0,1:T(8,128)}, u32[]{:S(2)}) copy-start(s32[64,8]{0,1:T(8,128)} %param.7) | copy-start | bytes 6148
  80.3 7.0 %copy-start.2 = (f32[64,8]{0,1:T(8,128)S(1)}, f32[64,8]{0,1:T(8,128)}, u32[]{:S(2)}) copy-start(f32[64,8]{0,1:T(8,128)} %param.8) | copy-start | bytes 6148
  80.3 7.4 %copy-start.3 = (f32[8,128]{1,0:T(8,128)S(1)}, f32[8,128]{1,0:T(8,128)}, u32[]{:S(2)}) copy-start(f32[8,128]{1,0:T(8,128)} %get-tuple-element.12) | copy-start | bytes 12292
  80.3 52.8 %all-to-all-start.1 = ((bf16[128,8,1792]{2,1,0:T(8,128)(2,1)}), bf16[128,8,1792]{2,1,0:T(8,128)(2,1)}, u32[]{:S(2)}, u32[]{:S(2)}) async-start(bf16[128,8,1792]{2,1,0:T(8,128)(2,1)} %bitcast.27), calls=%async_computation.1 | async-start | bytes 7340032 | tf_op jit(solution)/shard_map/all_to_all | solution.py:269
  85.8 5.5 %collective-permute-start.4 = (bf16[512,1024]{1,0:T(8,128)(2,1)S(1)}, bf16[512,1024]{1,0:T(8,128)(2,1)S(1)}, u32[]{:S(2)}, u32[]{:S(2)}) collective-permute-start(bf16[512,1024]{1,0:T(8,128)(2,1)S(1)} %copy-done), channel_id=1, source_target_pairs={{0,1},{1,0},{2,3},{3,2},{4,5},{5,4},{6,7},{7,6},{8,9},{9,8},{10,11... | collective-permute-start | bytes 3145736 | tf_op jit(solution)/shard_map/ppermute | solution.py:233
  87.6 1.8 %collective-permute-start.3 = (f32[8,128]{1,0:T(8,128)S(1)}, f32[8,128]{1,0:T(8,128)S(1)}, u32[]{:S(2)}, u32[]{:S(2)}) collective-permute-start(f32[8,128]{1,0:T(8,128)S(1)} %copy-done.3), channel_id=1, source_target_pairs={{0,1},{1,0},{2,3},{3,2},{4,5},{5,4},{6,7},{7,6},{8,9},{9,8},{10,11... | collective-permute-start | bytes 12296 | tf_op jit(solution)/shard_map/ppermute | solution.py:233

commit v6 on v5

--- a/solution.py
+++ b/solution.py
@@ -78,11 +78,11 @@
 
 
 def expert_kernel(
-    core_ref, x_hbm, gate_own, up_own, gate_other, up_other, down_own, down_other,
+    x_hbm, gate_own, up_own, gate_other, up_other, down_own, down_other,
     out_hbm, hid_hbm, count_hbm, x, first, second, outs, hid_ref, count_ref,
     x_sems, f_sems, s_sems, o_sems, e_sems,
 ):
-    core = core_ref[0]
+    core = lax.axis_index("token")
     _, groups, part, half = x.shape
     rows = groups * part
     ff_half = gate_own.shape[2]
@@ -192,7 +192,7 @@
         copy.wait()
 
 
-def run_experts(core, x, gate_own, up_own, gate_other, up_other, down_own, down_other):
+def run_experts(x, gate_own, up_own, gate_other, up_other, down_own, down_other):
     groups, _, part, half = x.shape
     rows = groups * part
     width = 2 * half
@@ -206,7 +206,7 @@
             jax.ShapeDtypeStruct((rows, ff), jnp.bfloat16),
             jax.ShapeDtypeStruct((8, 128), jnp.float32),
         ),
-        in_specs=[pl.BlockSpec(memory_space=pltpu.SMEM)] + [far] * 7,
+        in_specs=[far] * 7,
         out_specs=(far, far, far),
         scratch_shapes=[
             pltpu.VMEM((2, groups, part, half), jnp.bfloat16),
@@ -226,7 +226,7 @@
             flops=2 * rows * width * ff * 3, bytes_accessed=6 * width * ff + 4 * rows * width,
             transcendentals=rows * ff,
         ),
-    )(core, x, gate_own, up_own, gate_other, up_other, down_own, down_other)
+    )(x, gate_own, up_own, gate_other, up_other, down_own, down_other)
 
 
 def swap(array):
@@ -259,12 +259,9 @@
     outgoing = place_rows(routes.T, tokens, experts, part).reshape(2 * experts, part, half)
     received = lax.all_to_all(outgoing, ("expert", "token"), 0, 0, tiled=True)
     x = received.reshape(experts, 2, part, half)
-    _, gate_sent, up_sent, down_sent = lax.optimization_barrier(
-        (outgoing, gate_weight, up_weight, down_weight)
-    )
-    gate_other, up_other, down_other = swap(gate_sent), swap(up_sent), swap(down_sent)
+    gate_other, up_other, down_other = swap(gate_weight), swap(up_weight), swap(down_weight)
     out, hidden, count = run_experts(
-        core.reshape(1), x, gate_weight, up_weight, gate_other, up_other, down_weight, down_other
+        x, gate_weight, up_weight, gate_other, up_other, down_weight, down_other
     )
     returned = lax.all_to_all(
         out.reshape(2 * experts, part, half), ("expert", "token"), 0, 0, tiled=True

time: 137 us -> 137 us (level)
  blocking collectives: 0 us -> 57.8 us
  waiting for transfers between devices: 86.6 us -> 39.4 us
  starting transfers between devices: 19.5 us -> 8.97 us
    all_to_all x0 -> x1, blocking collectives: none -> 57.8 us  [shards(): received = lax.all_to_all(outgoing, ('expert', 'token'), 0, 0, tiled=True)]
    all_to_all x1 -> x0, waiting for transfers between devices: 47.1 us -> none  [shards(): received = lax.all_to_all(outgoing, ('expert', 'token'), 0, 0, tiled=True)]
    all_to_all x1 -> x0, starting transfers between devices: 10.6 us -> none  [shards(): received = lax.all_to_all(outgoing, ('expert', 'token'), 0, 0, tiled=True)]
  transfers between devices with their start and end apart: 7 -> 6, of which waited for: 3 -> 2; matrix products, arithmetic and copies ran while one was open for 4% -> 4% of each run, Pallas kernels for 0% -> 2%
where the time goes in v6:
time: 137 us
  blocking collectives  57.8 us (42%)
  waiting for transfers between devices  39.4 us (29%)
  Pallas kernels  19.8 us (14%)
  starting transfers between devices  8.97 us (7%)
  matrix products  5.79 us (4%)
  between operations  2.09 us (2%)
  local copies, waits for them, and re-layouts  1.45 us (1%)
    all_to_all x1, blocking collectives, shards(): received = lax.all_to_all(outgoing, ('expert', 'token'), 0, 0, tiled=True)  57.8 us
    all_to_all x1, waiting for transfers between devices, shards(): lax.all_to_all(out.reshape(2 * experts, part, half), ('expert', 'token'),...  38.9 us
    pallas_call x1, Pallas kernels, run_experts(): pl.pallas_call(expert_kernel, out_shape=(jax.ShapeDtypeStruct((groups, 2,...  16.5 us
    all_to_all x1, starting transfers between devices, shards(): lax.all_to_all(out.reshape(2 * experts, part, half), ('expert', 'token'),...  5.53 us
    ppermute x5, starting transfers between devices, swap(): return lax.ppermute(array, 'token', [(0, 1), (1, 0)])  3.44 us
    pallas_call x1, Pallas kernels, place_rows(): pl.pallas_call(functools.partial(route_kernel, experts, part, wide), out_...  3.27 us
    dot_general x2, matrix products, outer(): lax.dot_general(own, array, (((0,), (0,)), ((), ())), preferred_element_t...  2.85 us
    dot_general x1, matrix products, shards(): jnp.dot(jnp.concatenate([high, low]), returned, preferred_element_type=jn...  2.8 us
  transfers between devices with their start and end apart: 6, of which 2 were waited for; matrix products, arithmetic and copies ran while one was open for 4% of the time, Pallas kernels for 2%

profile of v6, /device:TPU:1, one launch (start us, length us, event | category | flops | bytes accessed | tf_op | source)
XLA Modules:
  0.0 136.6 jit_solution(16398832833528289073)
XLA Ops:
  0.6 1.5 %collective-permute-start = (bf16[1,3584,512]{2,1,0:T(8,128)(2,1)}, bf16[1,3584,512]{2,1,0:T(8,128)(2,1)}, u32[]{:S(2)}, u32[]{:S(2)}) collective-permute-start(bf16[1,3584,512]{2,1,0:T(8,128)(2,1)} %gate_own.1), channel_id=1, source_target_pairs={{0,1},{1,0},{2,3},{3,2},{4,5},{5,4},{6,7},{7,6},{8,9},{9,8},{10,11... | collective-permute-start | bytes 11010056 | tf_op jit(solution)/shard_map/ppermute | solution.py:233
  2.1 0.1 collective-permute-start.1
  2.2 0.4 collective-permute-start.2
  2.6 3.3 %shard_map.77 = bf16[1024,1792]{1,0:T(8,128)(2,1)} custom-call(s32[8,64]{1,0:T(8,128)} %bitcast.28, bf16[64,1792]{1,0:T(8,128)(2,1)} %tokens_hbm.1), custom_call_target="tpu_custom_call" | custom-call | tf_op jit(solution)/shard_map/pallas_call | solution.py:65
  5.9 57.8 %all_to_all.10 = bf16[128,8,1792]{2,1,0:T(8,128)(2,1)} all-to-all(bf16[128,8,1792]{2,1,0:T(8,128)(2,1)} %bitcast.25), channel_id=1, replica_groups=mesh['expert'=64,'token'=2] {'expert','token'}, dimensions={0} | all-to-all | bytes 7340032 | tf_op jit(solution)/shard_map/all_to_all | solution.py:260
  63.7 0.0 collective-permute-done.gate_other
  63.7 0.0 collective-permute-done.1.up_other
  63.7 16.5 %shard_map.78 = (bf16[64,2,8,1792]{3,2,1,0:T(8,128)(2,1)}, bf16[512,1024]{1,0:T(8,128)(2,1)}, f32[8,128]{1,0:T(8,128)}) custom-call(bf16[64,2,8,1792]{3,2,1,0:T(8,128)(2,1)} %bitcast.27, bf16[1,3584,512]{2,1,0:T(8,128)(2,1)} %gate_own.1, bf16[1,3584,512]{2,1,0:T(8,128)(2,1)} %up_own.1, bf16[1,3584,512]{2,1,0:T(8,128)(2,1)} %collective-permute-done.gate_other, ...), custom_call_target="tpu_custom_call" | custom-call | flops 11274289152 | bytes 29360128 | tf_op jit(solution)/shard_map/pallas_call | solution.py:202
  80.2 0.0 copy-start
  80.2 0.0 copy-start.1
  80.2 0.0 copy-start.2
  80.3 0.0 copy-start.3
  80.3 5.5 %all-to-all-start.1 = ((bf16[128,8,1792]{2,1,0:T(8,128)(2,1)}), bf16[128,8,1792]{2,1,0:T(8,128)(2,1)}, u32[]{:S(2)}, u32[]{:S(2)}) async-start(bf16[128,8,1792]{2,1,0:T(8,128)(2,1)} %bitcast.26), calls=%async_computation.1 | async-start | bytes 7340032 | tf_op jit(solution)/shard_map/all_to_all | solution.py:266
  85.8 1.4 collective-permute-start.4
  87.2 0.1 copy.13
  87.3 0.1 copy.15
  87.3 0.2 fusion.14
  87.5 0.1 fusion.2
  87.7 0.1 collective-permute-start.3
  87.7 0.2 select_reduce_fusion
  88.0 0.1 copy.16
  88.0 0.1 eq.39
  88.1 0.1 copy.14
  88.2 0.2 reduce-precision_convert_fusion
  88.4 0.5 slice.14
  88.9 0.5 collective-permute-done.3
  89.5 0.5 slice.15
  91.3 0.8 fusion.4
  92.1 2.1 %multiply_bitcast_fusion = f32[1,512,1024]{2,1,0:T(8,128)} fusion(f32[512,1024]{1,0:T(8,128)S(1)} %fusion.4, f32[]{:T(128)} %bitcast.7, bf16[512,1024]{1,0:T(8,128)(2,1)S(1)} %copy-done, s32[]{:T(128)S(6)} %select_n.20), kind=kOutput, calls=%fused_computation.2 | convolution fusion | flops 537919488 | bytes 5767176 | tf_op jit(solution)/shard_map/dot_general | solution.py:274
  94.2 38.9 %all-to-all-done.1 = bf16[128,8,1792]{2,1,0:T(8,128)(2,1)} async-done(((bf16[128,8,1792]{2,1,0:T(8,128)(2,1)}), bf16[128,8,1792]{2,1,0:T(8,128)(2,1)}, u32[]{:S(2)}, u32[]{:S(2)}) %all-to-all-start.1) | async-done | bytes 3670048 | tf_op jit(solution)/shard_map/all_to_all | solution.py:266
  133.1 2.8 %fusion = f32[128,1792]{1,0:T(8,128)S(1)} fusion(bf16[128,8,1792]{2,1,0:T(8,128)(2,1)} %all-to-all-done.1, bf16[64,1024]{0,1:T(8,128)(2,1)S(1)} %get-tuple-element.9, bf16[64,1024]{0,1:T(8,128)(2,1)S(1)} %get-tuple-element.8), kind=kOutput, calls=%fused_computation | convolution fusion | flops 470286336 | bytes 4849664 | tf_op jit(solution)/shard_map/dot_general | solution.py:281
  135.9 0.7 fusion.10
  (7 shorter events, 0.0 us)
Async XLA Ops:
  0.6 63.1 %collective-permute-start = (bf16[1,3584,512]{2,1,0:T(8,128)(2,1)}, bf16[1,3584,512]{2,1,0:T(8,128)(2,1)}, u32[]{:S(2)}, u32[]{:S(2)}) collective-permute-start(bf16[1,3584,512]{2,1,0:T(8,128)(2,1)} %gate_own.1), channel_id=1, source_target_pairs={{0,1},{1,0},{2,3},{3,2},{4,5},{5,4},{6,7},{7,6},{8,9},{9,8},{10,11... | collective-permute-start | bytes 11010056 | tf_op jit(solution)/shard_map/ppermute | solution.py:233
  2.1 61.6 %collective-permute-start.1 = (bf16[1,3584,512]{2,1,0:T(8,128)(2,1)}, bf16[1,3584,512]{2,1,0:T(8,128)(2,1)}, u32[]{:S(2)}, u32[]{:S(2)}) collective-permute-start(bf16[1,3584,512]{2,1,0:T(8,128)(2,1)} %up_own.1), channel_id=1, source_target_pairs={{0,1},{1,0},{2,3},{3,2},{4,5},{5,4},{6,7},{7,6},{8,9},{9,8},{10,11... | collective-permute-start | bytes 11010056 | tf_op jit(solution)/shard_map/ppermute | solution.py:233
  2.2 61.5 %collective-permute-start.2 = (bf16[1,1024,1792]{2,1,0:T(8,128)(2,1)}, bf16[1,1024,1792]{2,1,0:T(8,128)(2,1)}, u32[]{:S(2)}, u32[]{:S(2)}) collective-permute-start(bf16[1,1024,1792]{2,1,0:T(8,128)(2,1)} %down_own.1), channel_id=1, source_target_pairs={{0,1},{1,0},{2,3},{3,2},{4,5},{5,4},{6,7},{7,6},{8,9},{9,8},{10,11... | collective-permute-start | bytes 11010056 | tf_op jit(solution)/shard_map/ppermute | solution.py:233
  80.2 5.6 %copy-start = (bf16[512,1024]{1,0:T(8,128)(2,1)S(1)}, bf16[512,1024]{1,0:T(8,128)(2,1)}, u32[]{:S(2)}) copy-start(bf16[512,1024]{1,0:T(8,128)(2,1)} %get-tuple-element.7) | copy-start | bytes 3145732
  80.2 6.9 %copy-start.1 = (s32[64,8]{0,1:T(8,128)S(1)}, s32[64,8]{0,1:T(8,128)}, u32[]{:S(2)}) copy-start(s32[64,8]{0,1:T(8,128)} %param.7) | copy-start | bytes 6148
  80.2 7.0 %copy-start.2 = (f32[64,8]{0,1:T(8,128)S(1)}, f32[64,8]{0,1:T(8,128)}, u32[]{:S(2)}) copy-start(f32[64,8]{0,1:T(8,128)} %param.8) | copy-start | bytes 6148
  80.3 7.4 %copy-start.3 = (f32[8,128]{1,0:T(8,128)S(1)}, f32[8,128]{1,0:T(8,128)}, u32[]{:S(2)}) copy-start(f32[8,128]{1,0:T(8,128)} %get-tuple-element.6) | copy-start | bytes 12292
  80.3 52.8 %all-to-all-start.1 = ((bf16[128,8,1792]{2,1,0:T(8,128)(2,1)}), bf16[128,8,1792]{2,1,0:T(8,128)(2,1)}, u32[]{:S(2)}, u32[]{:S(2)}) async-start(bf16[128,8,1792]{2,1,0:T(8,128)(2,1)} %bitcast.26), calls=%async_computation.1 | async-start | bytes 7340032 | tf_op jit(solution)/shard_map/all_to_all | solution.py:266
  85.8 5.5 %collective-permute-start.4 = (bf16[512,1024]{1,0:T(8,128)(2,1)S(1)}, bf16[512,1024]{1,0:T(8,128)(2,1)S(1)}, u32[]{:S(2)}, u32[]{:S(2)}) collective-permute-start(bf16[512,1024]{1,0:T(8,128)(2,1)S(1)} %copy-done), channel_id=1, source_target_pairs={{0,1},{1,0},{2,3},{3,2},{4,5},{5,4},{6,7},{7,6},{8,9},{9,8},{10,11... | collective-permute-start | bytes 3145736 | tf_op jit(solution)/shard_map/ppermute | solution.py:233
  87.7 1.8 %collective-permute-start.3 = (f32[8,128]{1,0:T(8,128)S(1)}, f32[8,128]{1,0:T(8,128)S(1)}, u32[]{:S(2)}, u32[]{:S(2)}) collective-permute-start(f32[8,128]{1,0:T(8,128)S(1)} %copy-done.3), channel_id=1, source_target_pairs={{0,1},{1,0},{2,3},{3,2},{4,5},{5,4},{6,7},{7,6},{8,9},{9,8},{10,11... | collective-permute-start | bytes 12296 | tf_op jit(solution)/shard_map/ppermute | solution.py:233
